TPU v7x, 32 devices: a whole 2x2x4 slice. The times are simulated.
32 devices in a mesh: grp: 2 (over y), slab: 4 (over x, core), row: 4 (over z).
Axes of the slice: x: 2, y: 2, z: 4, core: 2. Of those that a mesh axis runs over, the one named last changes fastest.
Arguments:
- velocity: float32 [3, 128, 16, 512], P(None, 'slab', 'grp', 'row'), may hold values from -6 to 6
- modes: float32 [24576, 512], P(('grp', 'slab', 'row')), may hold values from -6 to 6
- planes: int32 [64], replicated, may hold values from 0 to 127, as said below
- assign: int32 [4], replicated, may hold values from 0 to 3, each once
Outputs:
- advanced: float32 [3, 128, 16, 512], P(None, 'slab', 'grp', 'row')
- basis: float32 [24576, 576], P(('grp', 'slab', 'row'))
- factor: float32 [576, 576], replicated
Inputs may be any that keep to these rules, and one draw needn't show every extreme that they name: `planes`: the 64 plane indices are distinct.
All inputs are finite; a program needn't handle non-finite values.
Results may differ from a plain program's by a relative error of at most 0.00005.
Values sent between devices are 32-bit elements; how exact they have to be, the bound alone decides.
A program may use at most 64 MiB of HBM per device.

v0:
```python
import jax
import jax.numpy as jnp
from jax import lax
from jax.sharding import PartitionSpec as P

step_size = 0.05
viscosity = 1.0
third = 1.0 / 3.0
carry_back = -5.0 / 9.0
second_gain = 15.0 / 16.0


def padded(array, sides, width, wrap):
    for axis, dim in sides:
        devices, length = (lax.axis_size(axis), array.shape[dim])
        up = [(i, (i + 1) % devices) for i in range(devices if wrap else devices - 1)]
        down = [(j, i) for i, j in up]
        last = lax.slice_in_dim(array, length - width, length, axis=dim)
        initial = lax.slice_in_dim(array, 0, width, axis=dim)
        before = lax.ppermute(last, axis, up)
        after = lax.ppermute(initial, axis, down)
        array = jnp.concatenate([before, array, after], axis=dim)
    return array


def derivatives(parts):
    first = (parts[0] - 8.0 * parts[1] + 8.0 * parts[3] - parts[4]) / 12.0
    second = (-parts[0] + 16.0 * parts[1] - 30.0 * parts[2] + 16.0 * parts[3] - parts[4]) / 12.0
    return (first, second)


def tendency(field):
    wide = padded(field, (("grp", 2), ("slab", 1)), 2, True)
    walls = padded(field, (("row", 3),), 2, False)
    depth, across, height = (field.shape[1], field.shape[2], field.shape[3])
    along_z = [wide[:, k : k + depth, 2 : 2 + across, :] for k in range(5)]
    along_x = [wide[:, 2 : 2 + depth, k : k + across, :] for k in range(5)]
    along_y = [walls[:, :, :, k : k + height] for k in range(5)]
    dz_first, dz_second = derivatives(along_z)
    dx_first, dx_second = derivatives(along_x)
    dy_first, dy_second = derivatives(along_y)
    convect = field[0:1] * dx_first + field[1:2] * dy_first + field[2:3] * dz_first
    laplace = dx_second + dy_second + dz_second
    return viscosity * laplace - convect


def product(left, right):
    return jnp.dot(left, right, precision=lax.Precision.HIGHEST, preferred_element_type=jnp.float32)


def on_device(velocity, modes, planes, assign):
    count = planes.shape[0]
    slabs = lax.axis_size("slab")
    rows_total = modes.shape[0] * lax.axis_size("grp") * slabs * lax.axis_size("row")
    first_q = step_size * tendency(velocity)
    middle = velocity + third * first_q
    second_q = carry_back * first_q + step_size * tendency(middle)
    advanced = middle + second_gain * second_q
    depth = velocity.shape[1]
    local_z = planes - lax.axis_index("slab") * depth
    owned = (local_z >= 0) & (local_z < depth)
    picked = jnp.take(advanced, jnp.clip(local_z, 0, depth - 1), axis=1)
    picked = jnp.where(owned[None, :, None, None], picked, 0.0)
    picked = jnp.transpose(picked, (1, 0, 2, 3)).reshape(count, slabs, -1)
    arranged = jnp.take(picked, assign, axis=1)
    received = lax.psum_scatter(
        arranged.reshape(count, -1), "slab", scatter_dimension=1, tiled=True
    )
    snapshot_rows = received.T
    joined = jnp.concatenate([modes, snapshot_rows], axis=1)
    summed = lax.psum(product(joined.T, joined), ("grp", "slab", "row"))
    gram = summed / float(rows_total)
    lower = jnp.linalg.cholesky(gram)
    basis = jax.scipy.linalg.solve_triangular(lower, joined.T, lower=True).T
    return (advanced, basis, lower.T)


def solution(mesh):
    placed = (P(None, "slab", "grp", "row"), P(("grp", "slab", "row"), None), P(), P())
    return jax.shard_map(
        on_device,
        mesh=mesh,
        in_specs=placed,
        out_specs=(P(None, "slab", "grp", "row"), P(("grp", "slab", "row"), None), P()),
        check_vma=False,
    )
```

profile of v0, /device:TPU:0, one launch (start us, length us, event | category | flops | bytes accessed | tf_op | source)
XLA Modules:
  0.0 424.3 jit_solution(11740263624295712779)
XLA Ops:
  8.5 3.0 collective-permute-start
  13.7 3.9 collective-permute-start.2
  21.0 8.7 %collective-permute-done.3 = f32[3,32,8,2]{3,2,1,0:T(8,128)S(1)} collective-permute-done((f32[3,32,8,2]{3,2,1,0:T(8,128)}, f32[3,32,8,2]{3,2,1,0:T(8,128)S(1)}, u32[]{:S(2)}, u32[]{:S(2)}) %collective-permute-start.3) | collective-permute-done | bytes 6176 | tf_op jit(solution)/shard_map/ppermute | solution.py:21
  36.8 3.5 collective-permute-start.8
  43.6 6.0 %collective-permute-done.8 = f32[3,32,8,2]{3,2,1,0:T(8,128)S(1)} collective-permute-done((f32[3,32,8,2]{3,2,1,0:T(8,128)S(1)}, f32[3,32,8,2]{3,2,1,0:T(8,128)S(1)}, u32[]{:S(2)}, u32[]{:S(2)}) %collective-permute-start.8) | collective-permute-done | bytes 6176 | tf_op jit(solution)/shard_map/ppermute | solution.py:20
  49.6 4.3 %collective-permute-done.9 = f32[3,32,8,2]{3,2,1,0:T(8,128)S(1)} collective-permute-done((f32[3,32,8,2]{3,2,1,0:T(8,128)S(1)}, f32[3,32,8,2]{3,2,1,0:T(8,128)S(1)}, u32[]{:S(2)}, u32[]{:S(2)}) %collective-permute-start.9) | collective-permute-done | bytes 6176 | tf_op jit(solution)/shard_map/ppermute | solution.py:21
  59.5 20.5 %reduce-scatter.2.cloned.1.call-done = f32[64,768]{1,0:T(8,128)} async-done(((f32[64,3072]{1,0:T(8,128)}), f32[64,768]{1,0:T(8,128)}) %reduce-scatter.2.cloned.1.call-update) | async-done | bytes 196624 | tf_op jit(solution)/shard_map/reduce_scatter | solution.py:66
  80.0 6.5 %fusion.11 = f32[576,576]{0,1:T(8,128)} fusion(f32[768,64]{0,1:T(8,128)} %bitcast.92, f32[768,512]{0,1:T(8,128)S(1)} %copy.16), kind=kOutput, calls=%fused_computation.19 | convolution fusion | flops 3058089984 | bytes 3096576 | tf_op jit(solution)/shard_map/dot_general | solution.py:48
  87.6 130.1 %all-reduce.5.cloned.1.call-done = f32[576,576]{0,1:T(8,128)} async-done(((f32[576,576]{0,1:T(8,128)}), f32[576,576]{0,1:T(8,128)}) %all-reduce.5.cloned.1.call-update) | async-done | bytes 1327120 | tf_op jit(solution)/shard_map/psum | solution.py:71
  217.7 2.6 broadcast_multiply_fusion
  220.3 3.1 copy.18
  226.1 11.7 %cholesky.134 = f32[128,128]{1,0:T(8,128)S(1)} custom-call(f32[128,128]{1,0:T(8,128)S(1)} %cholesky.346), custom_call_target="Cholesky" | custom-call | tf_op jit(solution)/shard_map/jit(cholesky)/cholesky | solution.py:73
  237.8 9.8 %custom-call.39 = f32[1,128,128]{1,2,0:T(8,128)S(1)} custom-call(f32[1,128,128]{2,1,0:T(8,128)S(1)} %get-tuple-element.66), custom_call_target="InvertDiagBlocksLowerTriangular" | custom-call | tf_op jit(solution)/shard_map/jit(cholesky)/cholesky | solution.py:73
  251.2 13.2 %cholesky.274 = f32[128,128]{1,0:T(8,128)} custom-call(f32[128,128]{1,0:T(8,128)} %cholesky.350), custom_call_target="Cholesky" | custom-call | tf_op jit(solution)/shard_map/jit(cholesky)/cholesky | solution.py:73
  265.9 11.3 %custom-call.40 = f32[1,128,128]{1,2,0:T(8,128)} custom-call(f32[1,128,128]{2,1,0:T(8,128)} %get-tuple-element.63), custom_call_target="InvertDiagBlocksLowerTriangular" | custom-call | tf_op jit(solution)/shard_map/jit(cholesky)/cholesky | solution.py:73
  279.6 12.3 %cholesky.295 = f32[128,128]{1,0:T(8,128)} custom-call(f32[128,128]{1,0:T(8,128)S(1)} %cholesky.355), custom_call_target="Cholesky" | custom-call | tf_op jit(solution)/shard_map/jit(cholesky)/cholesky | solution.py:73
  293.5 10.8 %custom-call.41 = f32[1,128,128]{1,2,0:T(8,128)} custom-call(f32[1,128,128]{2,1,0:T(8,128)S(1)} %get-tuple-element.60), custom_call_target="InvertDiagBlocksLowerTriangular" | custom-call | tf_op jit(solution)/shard_map/jit(cholesky)/cholesky | solution.py:73
  306.7 11.7 %cholesky.314 = f32[128,128]{1,0:T(8,128)S(1)} custom-call(f32[128,128]{1,0:T(8,128)S(1)} %cholesky.360), custom_call_target="Cholesky" | custom-call | tf_op jit(solution)/shard_map/jit(cholesky)/cholesky | solution.py:73
  319.2 9.8 %custom-call.42 = f32[1,128,128]{1,2,0:T(8,128)S(1)} custom-call(f32[1,128,128]{2,1,0:T(8,128)S(1)} %get-tuple-element.57), custom_call_target="InvertDiagBlocksLowerTriangular" | custom-call | tf_op jit(solution)/shard_map/jit(cholesky)/cholesky | solution.py:73
  330.2 5.8 %cholesky.334 = f32[64,64]{1,0:T(8,128)S(1)} custom-call(f32[64,64]{1,0:T(8,128)S(1)} %convolution_subtract_fusion.6), custom_call_target="Cholesky" | custom-call | tf_op jit(solution)/shard_map/jit(cholesky)/cholesky | solution.py:73
  342.3 3.0 copy.19
  346.0 11.8 %while.1 = (s32[]{:T(128)}, f32[576,576]{1,0:T(8,128)}, s32[4,2]{0,1:T(2,128)S(1)}, f32[4,128,128]{2,1,0:T(8,128)S(1)}, s32[]{:T(128)}) while((s32[]{:T(128)}, f32[576,576]{1,0:T(8,128)}, s32[4,2]{0,1:T(2,128)S(1)}, f32[4,128,128]{2,1,0:T(8,128)S(1)}, s32[]{:T(128)}) %tuple.62), condition=%wide.while_cond, body=%wide.while_body.sunk | while | flops 2 | bytes 131189 | solution.py:74
  346.8 2.3 bitcast_dynamic-update-slice_fusion.2
  357.9 49.1 %custom-call.43 = f32[5,128,128]{1,2,0:T(8,128)S(1)} custom-call(f32[5,128,128]{2,1,0:T(8,128)S(1)} %pad_maximum_fusion.24), custom_call_target="InvertDiagBlocksLowerTriangular" | custom-call | tf_op jit(solution)/shard_map/jit(_solve_triangular)/triangular_solve | solution.py:74
  (125 shorter events, 63.1 us)
Async XLA Ops:
  7.2 12.4 %copy-start = (f32[3,32,8,128]{3,2,1,0:T(8,128)S(1)}, f32[3,32,8,128]{3,2,1,0:T(8,128)}, u32[]{:S(2)}) copy-start(f32[3,32,8,128]{3,2,1,0:T(8,128)} %param.4) | copy-start | bytes 1179652
  7.2 11.7 %copy-start.10 = (s32[4]{0:T(128)S(1)}, s32[4]{0:T(128)}, u32[]{:S(2)}) copy-start(s32[4]{0:T(128)} %param.7) | copy-start | bytes 52
  7.2 72.8 %reduce-scatter.2.cloned.1.call-start = ((), (), s32[]{:S(2)}) async-start(), calls=%async_computation.1 | async-start | bytes 983040 | tf_op jit(solution)/shard_map/reduce_scatter | solution.py:66
  8.5 21.3 %collective-permute-start = (f32[3,32,2,128]{3,2,1,0:T(2,128)S(1)}, f32[3,32,2,128]{3,2,1,0:T(2,128)S(1)}, u32[]{:S(2)}, u32[]{:S(2)}) collective-permute-start(f32[3,32,2,128]{3,2,1,0:T(2,128)S(1)} %get-tuple-element.51), channel_id=1, source_target_pairs={{0,16},{16,0},{1,17},{17,1},{2,18},{18,2},{3,19},{19,3},{4,20},{20... | collective-permute-start | bytes 294920 | tf_op jit(solution)/shard_map/ppermute | solution.py:20
  11.5 8.2 %copy-start.9 = (s32[64]{0:T(128)S(1)}, s32[64]{0:T(128)}, u32[]{:S(2)}) copy-start(s32[64]{0:T(128)} %param.6) | copy-start | bytes 772
  11.5 18.3 %collective-permute-start.1 = (f32[3,32,2,128]{3,2,1,0:T(2,128)S(1)}, f32[3,32,2,128]{3,2,1,0:T(2,128)S(1)}, u32[]{:S(2)}, u32[]{:S(2)}) collective-permute-start(f32[3,32,2,128]{3,2,1,0:T(2,128)S(1)} %get-tuple-element.52), channel_id=1, source_target_pairs={{16,0},{0,16},{17,1},{1,17},{18,2},{2,18},{19,3},{3,19},{20,4},{4,... | collective-permute-start | bytes 294920 | tf_op jit(solution)/shard_map/ppermute | solution.py:21
  13.7 18.0 %collective-permute-start.2 = (f32[3,32,8,2]{3,2,1,0:T(8,128)}, f32[3,32,8,2]{3,2,1,0:T(8,128)S(1)}, u32[]{:S(2)}, u32[]{:S(2)}) collective-permute-start(f32[3,32,8,2]{3,2,1,0:T(8,128)} %get-tuple-element.49), channel_id=1, source_target_pairs={{0,1},{1,2},{2,3},{4,5},{5,6},{6,7},{8,9},{9,10},{10,11},{12,13},{... | collective-permute-start | bytes 18440 | tf_op jit(solution)/shard_map/ppermute | solution.py:20
  17.6 12.1 %collective-permute-start.3 = (f32[3,32,8,2]{3,2,1,0:T(8,128)}, f32[3,32,8,2]{3,2,1,0:T(8,128)S(1)}, u32[]{:S(2)}, u32[]{:S(2)}) collective-permute-start(f32[3,32,8,2]{3,2,1,0:T(8,128)} %get-tuple-element.50), channel_id=1, source_target_pairs={{1,0},{2,1},{3,2},{5,4},{6,5},{7,6},{9,8},{10,9},{11,10},{13,12},{... | collective-permute-start | bytes 18440 | tf_op jit(solution)/shard_map/ppermute | solution.py:21
  29.8 3.6 collective-permute-start.4
  29.9 3.5 collective-permute-start.5
  34.5 7.1 %collective-permute-start.6 = (f32[3,32,2,128]{3,2,1,0:T(2,128)S(1)}, f32[3,32,2,128]{3,2,1,0:T(2,128)S(1)}, u32[]{:S(2)}, u32[]{:S(2)}) collective-permute-start(f32[3,32,2,128]{3,2,1,0:T(2,128)S(1)} %get-tuple-element.45), channel_id=1, source_target_pairs={{0,16},{16,0},{1,17},{17,1},{2,18},{18,2},{3,19},{19,3},{4,20},{20... | collective-permute-start | bytes 294920 | tf_op jit(solution)/shard_map/ppermute | solution.py:20
  36.1 5.7 %collective-permute-start.7 = (f32[3,32,2,128]{3,2,1,0:T(2,128)S(1)}, f32[3,32,2,128]{3,2,1,0:T(2,128)S(1)}, u32[]{:S(2)}, u32[]{:S(2)}) collective-permute-start(f32[3,32,2,128]{3,2,1,0:T(2,128)S(1)} %get-tuple-element.46), channel_id=1, source_target_pairs={{16,0},{0,16},{17,1},{1,17},{18,2},{2,18},{19,3},{3,19},{20,4},{4,... | collective-permute-start | bytes 294920 | tf_op jit(solution)/shard_map/ppermute | solution.py:21
  36.8 12.9 %collective-permute-start.8 = (f32[3,32,8,2]{3,2,1,0:T(8,128)S(1)}, f32[3,32,8,2]{3,2,1,0:T(8,128)S(1)}, u32[]{:S(2)}, u32[]{:S(2)}) collective-permute-start(f32[3,32,8,2]{3,2,1,0:T(8,128)S(1)} %get-tuple-element.43), channel_id=1, source_target_pairs={{0,1},{1,2},{2,3},{4,5},{5,6},{6,7},{8,9},{9,10},{10,11},{12,13},{... | collective-permute-start | bytes 18440 | tf_op jit(solution)/shard_map/ppermute | solution.py:20
  40.3 13.7 %collective-permute-start.9 = (f32[3,32,8,2]{3,2,1,0:T(8,128)S(1)}, f32[3,32,8,2]{3,2,1,0:T(8,128)S(1)}, u32[]{:S(2)}, u32[]{:S(2)}) collective-permute-start(f32[3,32,8,2]{3,2,1,0:T(8,128)S(1)} %get-tuple-element.44), channel_id=1, source_target_pairs={{1,0},{2,1},{3,2},{5,4},{6,5},{7,6},{9,8},{10,9},{11,10},{13,12},{... | collective-permute-start | bytes 18440 | tf_op jit(solution)/shard_map/ppermute | solution.py:21
  41.8 12.2 %collective-permute-start.10 = (f32[3,2,12,128]{3,2,1,0:T(8,128)S(1)}, f32[3,2,12,128]{3,2,1,0:T(8,128)S(1)}, u32[]{:S(2)}, u32[]{:S(2)}) collective-permute-start(f32[3,2,12,128]{3,2,1,0:T(8,128)S(1)} %get-tuple-element.36), channel_id=1, source_target_pairs={{0,4},{4,8},{8,12},{12,0},{1,5},{5,9},{9,13},{13,1},{2,6},{6,10},{... | collective-permute-start | bytes 110600 | tf_op jit(solution)/shard_map/ppermute | solution.py:20
  42.4 11.5 %collective-permute-start.11 = (f32[3,2,12,128]{3,2,1,0:T(8,128)S(1)}, f32[3,2,12,128]{3,2,1,0:T(8,128)S(1)}, u32[]{:S(2)}, u32[]{:S(2)}) collective-permute-start(f32[3,2,12,128]{3,2,1,0:T(8,128)S(1)} %get-tuple-element.37), channel_id=1, source_target_pairs={{4,0},{8,4},{12,8},{0,12},{5,1},{9,5},{13,9},{1,13},{6,2},{10,6},{... | collective-permute-start | bytes 110600 | tf_op jit(solution)/shard_map/ppermute | solution.py:21
  53.9 2.0 copy-start.7
  53.9 2.0 copy-start.8
  57.3 1.7 copy-start.4
  58.3 159.4 %all-reduce.5.cloned.1.call-start = ((), (), s32[]{:S(2)}) async-start(), calls=%async_computation.2 | async-start | bytes 2949120 | tf_op jit(solution)/shard_map/psum | solution.py:71
  220.3 3.1 copy-start.1
  225.0 1.1 copy-start.2
  342.2 3.8 copy-start.5
  416.1 1.2 copy-start.6
  (1 other events, 0.9 us)
Sparse Core Ops, SparseCore 0:
  58.4 21.5 reduce-scatter.1
  86.7 130.9 all-reduce.4
where the time goes:
time: 430 us; the launch traced here: 424 us
  waiting for transfers between devices  172 us (40%)
  other arithmetic  163 us (38%)
  local copies, waits for them, and re-layouts  28.7 us (7%)
  matrix products  24.3 us (6%)
  starting transfers between devices  19 us (4%)
  between operations  17.9 us (4%)
    psum x1, waiting for transfers between devices, on_device(): summed = lax.psum(product(joined.T, joined), ('grp', 'slab', 'row'))  130 us
    another operation x18, other arithmetic, on_device(): lower = jnp.linalg.cholesky(gram)  102 us
    another operation x6, other arithmetic, on_device(): basis = jax.scipy.linalg.solve_triangular(lower, joined.T, lower=True).T  49.3 us
    reduce_scatter x1, waiting for transfers between devices, on_device(): lax.psum_scatter(arranged.reshape(count, -1), 'slab', scatter_dimension=1...  20.5 us
    ppermute x6, waiting for transfers between devices, padded(): after = lax.ppermute(initial, axis, down)  13.2 us
    ppermute x6, starting transfers between devices, padded(): before = lax.ppermute(last, axis, up)  12.7 us
    another operation x12, local copies, waits for them, and re-layouts  11.5 us
    another operation x9, matrix products, on_device(): basis = jax.scipy.linalg.solve_triangular(lower, joined.T, lower=True).T  8.99 us
  transfers between devices with their start and end apart: 14, of which 7 were waited for; matrix products, arithmetic and copies ran while one was open for 1% of the time, Pallas kernels for 0%

commit v1 on v0

--- a/solution.py
+++ b/solution.py
@@ -1,6 +1,10 @@
+import functools
+
 import jax
 import jax.numpy as jnp
 from jax import lax
+from jax.experimental import pallas as pl
+from jax.experimental.pallas import tpu as pltpu
 from jax.sharding import PartitionSpec as P
 
 step_size = 0.05
@@ -8,6 +12,8 @@
 third = 1.0 / 3.0
 carry_back = -5.0 / 9.0
 second_gain = 15.0 / 16.0
+EDGE = 128
+PANEL = 8
 
 
 def padded(array, sides, width, wrap):
@@ -44,8 +50,120 @@
     return viscosity * laplace - convect
 
 
-def product(left, right):
-    return jnp.dot(left, right, precision=lax.Precision.HIGHEST, preferred_element_type=jnp.float32)
+def product(left, right, dims=((1,), (0,))):
+    return lax.dot_general(
+        left, right, (dims, ((), ())),
+        precision=lax.Precision.HIGHEST, preferred_element_type=jnp.float32,
+    )
+
+
+def eliminate(tile, factor_ref, inverse_ref):
+    size = tile.shape[0]
+    lane = lax.broadcasted_iota(jnp.int32, (PANEL, size), 1)
+    sub = lax.broadcasted_iota(jnp.int32, (PANEL, size), 0)
+    groups = [tile[PANEL * g : PANEL * (g + 1), :] for g in range(size // PANEL)]
+    for p in range(size // PANEL):
+        start = PANEL * p
+        own = groups[p]
+        inside = (lane >= start) & (lane < start + PANEL)
+        columns = [
+            jnp.broadcast_to(own[:, start + k : start + k + 1], own.shape) for k in range(PANEL)
+        ]
+        direct = own
+        unit = jnp.where(inside, jnp.where(lane - start == sub, 1.0, 0.0), own)
+        factor_rows = jnp.zeros_like(own)
+        inverse_rows = jnp.zeros_like(own)
+        for k in range(PANEL):
+            pivot = columns[k][k : k + 1, :]
+            root = lax.rsqrt(pivot)
+            scale = 1.0 / pivot
+            here = sub == k
+            row_direct, row_unit = direct[k : k + 1, :], unit[k : k + 1, :]
+            factor_rows = jnp.where(here, row_direct * root, factor_rows)
+            inverse_rows = jnp.where(here, row_unit * root, inverse_rows)
+            others = jnp.where(here, 0.0, columns[k])
+            for j in range(k + 1, PANEL):
+                row = columns[j][k : k + 1, :] * scale
+                columns[j] = jnp.where(here, row, columns[j]) - others * row
+            row = row_direct * scale
+            direct = jnp.where(here, row, direct) - others * row
+            row = row_unit * scale
+            unit = jnp.where(here, row, unit) - others * row
+        factor_ref[start : start + PANEL, :] = jnp.where(lane >= start + sub, factor_rows, 0.0)
+        inverse_ref[start : start + PANEL, :] = jnp.where(lane <= start + sub, inverse_rows, 0.0)
+        for g in range(p + 1, size // PANEL):
+            below = groups[g]
+            total = jnp.where(inside, 0.0, below)
+            for k in range(PANEL):
+                total = total - below[:, start + k : start + k + 1] * unit[k : k + 1, :]
+            groups[g] = total
+
+
+def factor_kernel(gram_ref, joined_ref, basis_ref, factor_ref, work, left, tile, upper, lower):
+    size = gram_ref.shape[0]
+    whole = work.shape[0]
+    blocks = whole // EDGE
+    work[...] = jnp.zeros_like(work)
+    work[:size, :size] = gram_ref[...]
+    tail = (blocks - 1) * EDGE
+    row = lax.broadcasted_iota(jnp.int32, (EDGE, EDGE), 0)
+    col = lax.broadcasted_iota(jnp.int32, (EDGE, EDGE), 1)
+    padding = (row == col) & (row + tail >= size)
+    work[tail:, tail:] = jnp.where(padding, 1.0, work[tail:, tail:])
+    left[...] = jnp.zeros_like(left)
+    left[:, :size] = joined_ref[...]
+    factor_ref[...] = jnp.zeros_like(factor_ref)
+
+    def step(k, carry):
+        for b in range(blocks):
+            @pl.when(k == b)
+            def _():
+                tile[...] = work[b * EDGE : (b + 1) * EDGE, b * EDGE : (b + 1) * EDGE]
+
+        eliminate(tile[...], upper, lower)
+        for b in range(blocks):
+            @pl.when(k == b)
+            def _():
+                low, high = b * EDGE, (b + 1) * EDGE
+                end = min(high, size)
+                inverse = lower[...]
+                solved = product(left[:, low:high], inverse, ((1,), (1,)))
+                basis_ref[:, low:end] = solved[:, : end - low]
+                factor_ref[low:end, low:end] = upper[: end - low, : end - low]
+                if high < whole:
+                    strip = product(inverse, work[low:high, high:])
+                    factor_ref[low:high, high:] = strip[:, : size - high]
+                    work[high:, high:] = work[high:, high:] - product(strip, strip, ((0,), (0,)))
+                    left[:, high:] = left[:, high:] - product(solved, strip)
+
+        return carry
+
+    lax.fori_loop(0, blocks, step, 0)
+
+
+def factorize(gram, joined):
+    size = gram.shape[0]
+    rows = joined.shape[0]
+    whole = -(-size // EDGE) * EDGE
+    vmem = pl.BlockSpec(memory_space=pltpu.VMEM)
+    return pl.pallas_call(
+        factor_kernel,
+        out_shape=(
+            jax.ShapeDtypeStruct((rows, size), jnp.float32),
+            jax.ShapeDtypeStruct((size, size), jnp.float32),
+        ),
+        in_specs=[vmem, vmem],
+        out_specs=(vmem, vmem),
+        scratch_shapes=[
+            pltpu.VMEM((whole, whole), jnp.float32),
+            pltpu.VMEM((rows, whole), jnp.float32),
+            pltpu.VMEM((EDGE, EDGE), jnp.float32),
+            pltpu.VMEM((EDGE, EDGE), jnp.float32),
+            pltpu.VMEM((EDGE, EDGE), jnp.float32),
+        ],
+        compiler_params=pltpu.CompilerParams(vmem_limit_bytes=40 * 1024 * 1024),
+        name="factorize",
+    )(gram, joined)
 
 
 def on_device(velocity, modes, planes, assign):
@@ -70,9 +188,8 @@
     joined = jnp.concatenate([modes, snapshot_rows], axis=1)
     summed = lax.psum(product(joined.T, joined), ("grp", "slab", "row"))
     gram = summed / float(rows_total)
-    lower = jnp.linalg.cholesky(gram)
-    basis = jax.scipy.linalg.solve_triangular(lower, joined.T, lower=True).T
-    return (advanced, basis, lower.T)
+    basis, factor = factorize(gram, joined)
+    return (advanced, basis, factor)
 
 
 def solution(mesh):

time: 430 us -> 264 us (0.61); the launches traced: 424 us -> 264 us
  other arithmetic: 163 us -> 8.91 us
  Pallas kernels: 0 us -> 26.6 us
  local copies, waits for them, and re-layouts: 28.7 us -> 10.7 us
  matrix products: 24.3 us -> 7.03 us
  waiting for transfers between devices: 172 us -> 177 us
    another operation x24 -> x0, other arithmetic: 151 us -> none  [the longest x18 102 us: on_device(): lower = jnp.linalg.cholesky(gram)]
    pallas_call x0 -> x1, Pallas kernels: none -> 26.6 us  [factorize(): pl.pallas_call(factor_kernel, out_shape=(jax.ShapeDtypeStruct((rows, size...]
    another operation x17 -> x0, matrix products: 17.8 us -> none  [the longest x9 8.99 us: on_device(): basis = jax.scipy.linalg.solve_triangular(lower, joined.T, lower=True).T]
    another operation x19 -> x0, local copies, waits for them, and re-layouts: 13 us -> none
    reduce_scatter x1, waiting for transfers between devices: 20.5 us -> 26.4 us  [on_device(): lax.psum_scatter(arranged.reshape(count, -1), 'slab', scatter_dimension=1...]
  transfers between devices with their start and end apart: 14 -> 14, of which waited for: 7 -> 7; matrix products, arithmetic and copies ran while one was open for 1% -> 2% of each run, Pallas kernels for 0% -> 0%
where the time goes in v1:
time: 264 us
  waiting for transfers between devices  177 us (67%)
  Pallas kernels  26.6 us (10%)
  starting transfers between devices  19 us (7%)
  between operations  14.3 us (5%)
  local copies, waits for them, and re-layouts  10.7 us (4%)
  other arithmetic  8.91 us (3%)
  matrix products  7.03 us (3%)
    psum x1, waiting for transfers between devices, on_device(): summed = lax.psum(product(joined.T, joined), ('grp', 'slab', 'row'))  130 us
    pallas_call x1, Pallas kernels, factorize(): pl.pallas_call(factor_kernel, out_shape=(jax.ShapeDtypeStruct((rows, size...  26.6 us
    reduce_scatter x1, waiting for transfers between devices, on_device(): lax.psum_scatter(arranged.reshape(count, -1), 'slab', scatter_dimension=1...  26.4 us
    ppermute x6, waiting for transfers between devices, padded(): after = lax.ppermute(initial, axis, down)  13.3 us
    ppermute x6, starting transfers between devices, padded(): before = lax.ppermute(last, axis, up)  12.7 us
    ppermute x6, waiting for transfers between devices, padded(): before = lax.ppermute(last, axis, up)  7.75 us
    dot_general x1, matrix products, product(): lax.dot_general(left, right, (dims, ((), ())), precision=lax.Precision.HI...  7.03 us
    ppermute x6, starting transfers between devices, padded(): after = lax.ppermute(initial, axis, down)  6.07 us
  transfers between devices with their start and end apart: 14, of which 7 were waited for; matrix products, arithmetic and copies ran while one was open for 2% of the time, Pallas kernels for 0%

profile of v1, /device:TPU:0, one launch (start us, length us, event | category | flops | bytes accessed | tf_op | source)
XLA Modules:
  0.0 263.9 jit_solution(6520981709249864495)
XLA Ops:
  7.2 1.2 fusion.21
  8.5 3.0 %collective-permute-start = (f32[3,32,2,128]{3,2,1,0:T(2,128)S(1)}, f32[3,32,2,128]{3,2,1,0:T(2,128)S(1)}, u32[]{:S(2)}, u32[]{:S(2)}) collective-permute-start(f32[3,32,2,128]{3,2,1,0:T(2,128)S(1)} %get-tuple-element.35), channel_id=1, source_target_pairs={{0,16},{16,0},{1,17},{17,1},{2,18},{18,2},{3,19},{19,3},{4,20},{20... | collective-permute-start | bytes 294920 | tf_op jit(solution)/shard_map/ppermute | solution.py:26
  11.6 2.1 fusion.20
  13.7 3.9 %collective-permute-start.2 = (f32[3,32,8,2]{3,2,1,0:T(8,128)}, f32[3,32,8,2]{3,2,1,0:T(8,128)S(1)}, u32[]{:S(2)}, u32[]{:S(2)}) collective-permute-start(f32[3,32,8,2]{3,2,1,0:T(8,128)} %get-tuple-element.33), channel_id=1, source_target_pairs={{0,1},{1,2},{2,3},{4,5},{5,6},{6,7},{8,9},{9,10},{10,11},{12,13},{... | collective-permute-start | bytes 18440 | tf_op jit(solution)/shard_map/ppermute | solution.py:26
  17.6 1.3 collective-permute-start.3
  20.9 8.8 %collective-permute-done.3 = f32[3,32,8,2]{3,2,1,0:T(8,128)S(1)} collective-permute-done((f32[3,32,8,2]{3,2,1,0:T(8,128)}, f32[3,32,8,2]{3,2,1,0:T(8,128)S(1)}, u32[]{:S(2)}, u32[]{:S(2)}) %collective-permute-start.3) | collective-permute-done | bytes 6176 | tf_op jit(solution)/shard_map/ppermute | solution.py:27
  29.9 1.7 collective-permute-start.5
  31.7 1.7 collective-permute-done.4
  34.5 1.6 collective-permute-start.6
  36.8 3.5 %collective-permute-start.8 = (f32[3,32,8,2]{3,2,1,0:T(8,128)S(1)}, f32[3,32,8,2]{3,2,1,0:T(8,128)S(1)}, u32[]{:S(2)}, u32[]{:S(2)}) collective-permute-start(f32[3,32,8,2]{3,2,1,0:T(8,128)S(1)} %get-tuple-element.27), channel_id=1, source_target_pairs={{0,1},{1,2},{2,3},{4,5},{5,6},{6,7},{8,9},{9,10},{10,11},{12,13},{... | collective-permute-start | bytes 18440 | tf_op jit(solution)/shard_map/ppermute | solution.py:26
  40.3 1.3 collective-permute-start.9
  42.4 1.2 collective-permute-start.11
  43.6 6.0 %collective-permute-done.8 = f32[3,32,8,2]{3,2,1,0:T(8,128)S(1)} collective-permute-done((f32[3,32,8,2]{3,2,1,0:T(8,128)S(1)}, f32[3,32,8,2]{3,2,1,0:T(8,128)S(1)}, u32[]{:S(2)}, u32[]{:S(2)}) %collective-permute-start.8) | collective-permute-done | bytes 6176 | tf_op jit(solution)/shard_map/ppermute | solution.py:26
  49.7 4.3 %collective-permute-done.9 = f32[3,32,8,2]{3,2,1,0:T(8,128)S(1)} collective-permute-done((f32[3,32,8,2]{3,2,1,0:T(8,128)S(1)}, f32[3,32,8,2]{3,2,1,0:T(8,128)S(1)}, u32[]{:S(2)}, u32[]{:S(2)}) %collective-permute-start.9) | collective-permute-done | bytes 6176 | tf_op jit(solution)/shard_map/ppermute | solution.py:27
  54.0 1.3 fusion.9
  57.7 2.5 bitcast_select_fusion
  60.4 26.4 %reduce-scatter.2.cloned.1.call-done = f32[64,768]{0,1:T(8,128)} async-done(((f32[64,3072]{0,1:T(8,128)}), f32[64,768]{0,1:T(8,128)}) %reduce-scatter.2.cloned.1.call-update) | async-done | bytes 196624 | tf_op jit(solution)/shard_map/reduce_scatter | solution.py:184
  86.8 7.0 %fusion.17 = f32[576,576]{1,0:T(8,128)} fusion(f32[768,64]{1,0:T(8,128)} %bitcast.19, f32[768,512]{1,0:T(8,128)S(1)} %copy-done.3), kind=kOutput, calls=%fused_computation.85 | convolution fusion | flops 3058089984 | bytes 3096576 | tf_op jit(solution)/shard_map/dot_general | solution.py:54
  93.9 1.2 pad_maximum_fusion.joined_ref
  95.0 129.9 %all-reduce.2.cloned.1.call-done = f32[576,576]{1,0:T(8,128)} async-done(((f32[576,576]{1,0:T(8,128)}), f32[576,576]{1,0:T(8,128)}) %all-reduce.2.cloned.1.call-update) | async-done | bytes 1327120 | tf_op jit(solution)/shard_map/psum | solution.py:189
  225.0 1.5 broadcast_multiply_fusion.gram_ref
  226.5 26.6 %factorize.1 = (f32[768,576]{1,0:T(8,128)S(1)}, f32[576,576]{1,0:T(8,128)}) custom-call(f32[576,576]{1,0:T(8,128)S(1)} %broadcast_multiply_fusion.gram_ref, f32[768,576]{1,0:T(8,128)S(1)} %pad_maximum_fusion.joined_ref), custom_call_target="tpu_custom_call" | custom-call | tf_op jit(solution)/shard_map/factorize/pallas_call | solution.py:149
  253.1 1.3 copy-done
  254.4 2.8 %copy.12 = f32[768,576]{0,1:T(8,128)} copy(f32[768,576]{1,0:T(8,128)} %copy-done) | data formatting | bytes 3538944
  (54 shorter events, 7.6 us)
Async XLA Ops:
  7.2 12.3 %copy-start.1 = (f32[3,32,8,128]{3,2,1,0:T(8,128)S(1)}, f32[3,32,8,128]{3,2,1,0:T(8,128)}, u32[]{:S(2)}) copy-start(f32[3,32,8,128]{3,2,1,0:T(8,128)} %param.4) | copy-start | bytes 1179652
  7.2 11.7 %copy-start.7 = (s32[4]{0:T(128)S(1)}, s32[4]{0:T(128)}, u32[]{:S(2)}) copy-start(s32[4]{0:T(128)} %param.7) | copy-start | bytes 52
  7.2 79.6 %reduce-scatter.2.cloned.1.call-start = ((), (), s32[]{:S(2)}) async-start(), calls=%async_computation.1 | async-start | bytes 1966080 | tf_op jit(solution)/shard_map/reduce_scatter | solution.py:184
  8.5 21.3 %collective-permute-start = (f32[3,32,2,128]{3,2,1,0:T(2,128)S(1)}, f32[3,32,2,128]{3,2,1,0:T(2,128)S(1)}, u32[]{:S(2)}, u32[]{:S(2)}) collective-permute-start(f32[3,32,2,128]{3,2,1,0:T(2,128)S(1)} %get-tuple-element.35), channel_id=1, source_target_pairs={{0,16},{16,0},{1,17},{17,1},{2,18},{18,2},{3,19},{19,3},{4,20},{20... | collective-permute-start | bytes 294920 | tf_op jit(solution)/shard_map/ppermute | solution.py:26
  11.5 8.1 %copy-start.6 = (s32[64]{0:T(128)S(1)}, s32[64]{0:T(128)}, u32[]{:S(2)}) copy-start(s32[64]{0:T(128)} %param.6) | copy-start | bytes 772
  11.5 18.3 %collective-permute-start.1 = (f32[3,32,2,128]{3,2,1,0:T(2,128)S(1)}, f32[3,32,2,128]{3,2,1,0:T(2,128)S(1)}, u32[]{:S(2)}, u32[]{:S(2)}) collective-permute-start(f32[3,32,2,128]{3,2,1,0:T(2,128)S(1)} %get-tuple-element.36), channel_id=1, source_target_pairs={{16,0},{0,16},{17,1},{1,17},{18,2},{2,18},{19,3},{3,19},{20,4},{4,... | collective-permute-start | bytes 294920 | tf_op jit(solution)/shard_map/ppermute | solution.py:27
  13.7 18.0 %collective-permute-start.2 = (f32[3,32,8,2]{3,2,1,0:T(8,128)}, f32[3,32,8,2]{3,2,1,0:T(8,128)S(1)}, u32[]{:S(2)}, u32[]{:S(2)}) collective-permute-start(f32[3,32,8,2]{3,2,1,0:T(8,128)} %get-tuple-element.33), channel_id=1, source_target_pairs={{0,1},{1,2},{2,3},{4,5},{5,6},{6,7},{8,9},{9,10},{10,11},{12,13},{... | collective-permute-start | bytes 18440 | tf_op jit(solution)/shard_map/ppermute | solution.py:26
  17.6 12.1 %collective-permute-start.3 = (f32[3,32,8,2]{3,2,1,0:T(8,128)}, f32[3,32,8,2]{3,2,1,0:T(8,128)S(1)}, u32[]{:S(2)}, u32[]{:S(2)}) collective-permute-start(f32[3,32,8,2]{3,2,1,0:T(8,128)} %get-tuple-element.34), channel_id=1, source_target_pairs={{1,0},{2,1},{3,2},{5,4},{6,5},{7,6},{9,8},{10,9},{11,10},{13,12},{... | collective-permute-start | bytes 18440 | tf_op jit(solution)/shard_map/ppermute | solution.py:27
  29.8 3.6 %collective-permute-start.4 = (f32[3,2,12,128]{3,2,1,0:T(8,128)S(1)}, f32[3,2,12,128]{3,2,1,0:T(8,128)S(1)}, u32[]{:S(2)}, u32[]{:S(2)}) collective-permute-start(f32[3,2,12,128]{3,2,1,0:T(8,128)S(1)} %get-tuple-element.22), channel_id=1, source_target_pairs={{0,4},{4,8},{8,12},{12,0},{1,5},{5,9},{9,13},{13,1},{2,6},{6,10},{... | collective-permute-start | bytes 110600 | tf_op jit(solution)/shard_map/ppermute | solution.py:26
  29.9 3.5 %collective-permute-start.5 = (f32[3,2,12,128]{3,2,1,0:T(8,128)S(1)}, f32[3,2,12,128]{3,2,1,0:T(8,128)S(1)}, u32[]{:S(2)}, u32[]{:S(2)}) collective-permute-start(f32[3,2,12,128]{3,2,1,0:T(8,128)S(1)} %get-tuple-element.23), channel_id=1, source_target_pairs={{4,0},{8,4},{12,8},{0,12},{5,1},{9,5},{13,9},{1,13},{6,2},{10,6},{... | collective-permute-start | bytes 110600 | tf_op jit(solution)/shard_map/ppermute | solution.py:27
  34.5 7.1 %collective-permute-start.6 = (f32[3,32,2,128]{3,2,1,0:T(2,128)S(1)}, f32[3,32,2,128]{3,2,1,0:T(2,128)S(1)}, u32[]{:S(2)}, u32[]{:S(2)}) collective-permute-start(f32[3,32,2,128]{3,2,1,0:T(2,128)S(1)} %get-tuple-element.29), channel_id=1, source_target_pairs={{0,16},{16,0},{1,17},{17,1},{2,18},{18,2},{3,19},{19,3},{4,20},{20... | collective-permute-start | bytes 294920 | tf_op jit(solution)/shard_map/ppermute | solution.py:26
  36.1 5.7 %collective-permute-start.7 = (f32[3,32,2,128]{3,2,1,0:T(2,128)S(1)}, f32[3,32,2,128]{3,2,1,0:T(2,128)S(1)}, u32[]{:S(2)}, u32[]{:S(2)}) collective-permute-start(f32[3,32,2,128]{3,2,1,0:T(2,128)S(1)} %get-tuple-element.30), channel_id=1, source_target_pairs={{16,0},{0,16},{17,1},{1,17},{18,2},{2,18},{19,3},{3,19},{20,4},{4,... | collective-permute-start | bytes 294920 | tf_op jit(solution)/shard_map/ppermute | solution.py:27
  36.8 12.9 %collective-permute-start.8 = (f32[3,32,8,2]{3,2,1,0:T(8,128)S(1)}, f32[3,32,8,2]{3,2,1,0:T(8,128)S(1)}, u32[]{:S(2)}, u32[]{:S(2)}) collective-permute-start(f32[3,32,8,2]{3,2,1,0:T(8,128)S(1)} %get-tuple-element.27), channel_id=1, source_target_pairs={{0,1},{1,2},{2,3},{4,5},{5,6},{6,7},{8,9},{9,10},{10,11},{12,13},{... | collective-permute-start | bytes 18440 | tf_op jit(solution)/shard_map/ppermute | solution.py:26
  40.3 13.7 %collective-permute-start.9 = (f32[3,32,8,2]{3,2,1,0:T(8,128)S(1)}, f32[3,32,8,2]{3,2,1,0:T(8,128)S(1)}, u32[]{:S(2)}, u32[]{:S(2)}) collective-permute-start(f32[3,32,8,2]{3,2,1,0:T(8,128)S(1)} %get-tuple-element.28), channel_id=1, source_target_pairs={{1,0},{2,1},{3,2},{5,4},{6,5},{7,6},{9,8},{10,9},{11,10},{13,12},{... | collective-permute-start | bytes 18440 | tf_op jit(solution)/shard_map/ppermute | solution.py:27
  41.8 12.2 %collective-permute-start.10 = (f32[3,2,12,128]{3,2,1,0:T(8,128)S(1)}, f32[3,2,12,128]{3,2,1,0:T(8,128)S(1)}, u32[]{:S(2)}, u32[]{:S(2)}) collective-permute-start(f32[3,2,12,128]{3,2,1,0:T(8,128)S(1)} %get-tuple-element.20), channel_id=1, source_target_pairs={{0,4},{4,8},{8,12},{12,0},{1,5},{5,9},{9,13},{13,1},{2,6},{6,10},{... | collective-permute-start | bytes 110600 | tf_op jit(solution)/shard_map/ppermute | solution.py:26
  42.4 11.5 %collective-permute-start.11 = (f32[3,2,12,128]{3,2,1,0:T(8,128)S(1)}, f32[3,2,12,128]{3,2,1,0:T(8,128)S(1)}, u32[]{:S(2)}, u32[]{:S(2)}) collective-permute-start(f32[3,2,12,128]{3,2,1,0:T(8,128)S(1)} %get-tuple-element.21), channel_id=1, source_target_pairs={{4,0},{8,4},{12,8},{0,12},{5,1},{9,5},{13,9},{1,13},{6,2},{10,6},{... | collective-permute-start | bytes 110600 | tf_op jit(solution)/shard_map/ppermute | solution.py:27
  53.9 2.0 copy-start.4
  54.0 2.0 copy-start.5
  55.3 0.9 copy-start.2
  60.2 26.6 %copy-start.3 = (f32[768,512]{1,0:T(8,128)S(1)}, f32[768,512]{1,0:T(8,128)}, u32[]{:S(2)}) copy-start(f32[768,512]{1,0:T(8,128)} %param.5) | copy-start | bytes 4718596
  60.2 164.8 %all-reduce.2.cloned.1.call-start = ((), (), s32[]{:S(2)}) async-start(), calls=%async_computation.2 | async-start | bytes 2949120 | tf_op jit(solution)/shard_map/psum | solution.py:189
  253.1 1.3 copy-start
Sparse Core Ops, SparseCore 0:
  60.3 26.4 reduce-scatter.1
  94.0 130.9 all-reduce.1

commit v2 on v1

--- a/solution.py
+++ b/solution.py
@@ -99,19 +99,243 @@
             groups[g] = total
 
 
-def factor_kernel(gram_ref, joined_ref, basis_ref, factor_ref, work, left, tile, upper, lower):
-    size = gram_ref.shape[0]
+def wire_stages():
+    slabs = lax.axis_size("slab")
+    inner = 2 if slabs % 2 == 0 else 1
+    parts = [("slab", inner, slabs // inner), ("grp", 1, lax.axis_size("grp")), ("row", 1, lax.axis_size("row"))]
+    first = [("slab", 1, inner)]
+    return [first + parts[k:] + parts[:k] for k in range(3)]
+
+
+def place(stage):
+    axis, stride, members = stage
+    return lax.rem(lax.axis_index(axis) // stride, members)
+
+
+def peer(stage, distance):
+    axis, stride, members = stage
+    mine = place(stage)
+    other = lax.rem(mine + distance, members)
+    return {axis: lax.axis_index(axis) + (other - mine) * stride}, other
+
+
+def chunk_plan(rows, devices):
+    unit = PANEL * devices
+    units = rows // unit
+    orders = wire_stages()
+    chunks, base = [], 0
+    for c in range(3):
+        share = (units - sum(n for _, n, _ in chunks) + 2 - c) // (3 - c)
+        if share:
+            chunks.append((base * unit, share, orders[c]))
+            base += share
+    return [(start, share * unit, order) for start, share, order in chunks]
+
+
+def inbox_rows(chunks):
+    total = 0
+    for _, length, order in chunks:
+        for _, _, members in order:
+            length //= members
+            total += (members - 1) * length
+    return total
+
+
+def wire_count(chunks):
+    return 2 * sum(members - 1 for _, _, order in chunks for _, _, members in order)
+
+
+def combine_kernel(chunks, swap, *refs):
+    if swap:
+        part_ref, mine_ref, sum_ref, got_ref, acc, full, inbox, send, recv, got, swap_send, swap_recv = refs
+    else:
+        part_ref, sum_ref, acc, full, inbox, send, recv = refs
+    barrier = pltpu.get_barrier_semaphore()
+    stages = chunks[0][2]
+    slab = ("slab", 1, lax.axis_size("slab"))
+    greeted = [slab] + [st for st in stages if st[0] != "slab"] if swap else stages
+    total = 0
+    for stage in greeted:
+        for d in range(1, stage[2]):
+            pl.semaphore_signal(barrier, inc=1, device_id=peer(stage, d)[0], device_id_type=pl.DeviceIdType.MESH)
+            total += 1
+    acc[...] = part_ref[...]
+    pl.semaphore_wait(barrier, total)
+
+    count = 0
+    slot = 0
+    pending = []
+
+    def begin(source, target, device, index):
+        copy = pltpu.make_async_remote_copy(
+            src_ref=source, dst_ref=target, send_sem=send.at[index], recv_sem=recv.at[index],
+            device_id=device, device_id_type=pl.DeviceIdType.MESH,
+        )
+        copy.start()
+        pending.append(copy)
+        return copy
+
+    offsets = [jnp.int32(base) for base, _, _ in chunks]
+    lengths = [length for _, length, _ in chunks]
+    trail = [[] for _ in chunks]
+    swaps = []
+    for s in range(len(stages)):
+        started = []
+        for c, (_, _, order) in enumerate(chunks):
+            stage = order[s]
+            piece = lengths[c] // stage[2]
+            for d in range(1, stage[2]):
+                device, other = peer(stage, d)
+                source = acc.at[pl.ds(pl.multiple_of(offsets[c] + other * piece, PANEL), piece), :]
+                copy = begin(source, inbox.at[pl.ds(slot, piece), :], device, count)
+                started.append((c, copy, slot, piece))
+                count += 1
+                slot += piece
+        if swap and s == 0:
+            me = lax.axis_index("slab")
+            for d in range(1, slab[2]):
+                device, other = peer(slab, d)
+                copy = pltpu.make_async_remote_copy(
+                    src_ref=mine_ref.at[other], dst_ref=got.at[me],
+                    send_sem=swap_send.at[d - 1], recv_sem=swap_recv.at[d - 1],
+                    device_id=device, device_id_type=pl.DeviceIdType.MESH,
+                )
+                copy.start()
+                swaps.append(copy)
+        for c, (_, _, order) in enumerate(chunks):
+            stage = order[s]
+            piece = lengths[c] // stage[2]
+            trail[c].append((offsets[c], lengths[c]))
+            offsets[c] = pl.multiple_of(offsets[c] + place(stage) * piece, PANEL)
+            lengths[c] = piece
+            rows = pl.ds(offsets[c], piece)
+            for owner, copy, where, size in started:
+                if owner == c:
+                    copy.wait_recv()
+                    acc[rows, :] = acc[rows, :] + inbox[pl.ds(where, size), :]
+    for c in range(len(chunks)):
+        rows = pl.ds(offsets[c], lengths[c])
+        full[rows, :] = acc[rows, :]
+    for s in reversed(range(len(stages))):
+        started = []
+        for c, (_, _, order) in enumerate(chunks):
+            stage = order[s]
+            rows = pl.ds(offsets[c], lengths[c])
+            for d in range(1, stage[2]):
+                started.append(begin(full.at[rows, :], full.at[rows, :], peer(stage, d)[0], count))
+                count += 1
+            offsets[c], lengths[c] = trail[c][s]
+            offsets[c] = pl.multiple_of(offsets[c], PANEL)
+        for copy in started:
+            copy.wait_recv()
+    sum_ref[...] = full[...]
+    if swap:
+        for copy in swaps:
+            copy.wait_recv()
+        for j in range(slab[2]):
+            @pl.when(lax.axis_index("slab") == j)
+            def _():
+                got_ref[j] = mine_ref[j]
+
+            @pl.when(lax.axis_index("slab") != j)
+            def _():
+                got_ref[j] = got[j]
+    for copy in pending + swaps:
+        copy.wait_send()
+
+
+def combine(part, mine, collective_id):
+    devices = lax.axis_size("grp") * lax.axis_size("slab") * lax.axis_size("row")
+    chunks = chunk_plan(part.shape[0], devices)
+    swap = mine is not None
+    wires = wire_count(chunks)
+    vmem = pl.BlockSpec(memory_space=pltpu.VMEM)
+    out = [jax.ShapeDtypeStruct(part.shape, jnp.float32)]
+    scratch = [
+        pltpu.VMEM(part.shape, jnp.float32),
+        pltpu.VMEM(part.shape, jnp.float32),
+        pltpu.VMEM((inbox_rows(chunks), EDGE), jnp.float32),
+        pltpu.SemaphoreType.DMA((wires,)),
+        pltpu.SemaphoreType.DMA((wires,)),
+    ]
+    operands = [part]
+    if swap:
+        operands.append(mine)
+        out.append(jax.ShapeDtypeStruct(mine.shape, jnp.float32))
+        scratch += [
+            pltpu.VMEM(mine.shape, jnp.float32),
+            pltpu.SemaphoreType.DMA((mine.shape[0] - 1,)),
+            pltpu.SemaphoreType.DMA((mine.shape[0] - 1,)),
+        ]
+    return pl.pallas_call(
+        functools.partial(combine_kernel, chunks, swap),
+        out_shape=out,
+        in_specs=[vmem] * len(operands),
+        out_specs=[vmem] * len(out),
+        scratch_shapes=scratch,
+        compiler_params=pltpu.CompilerParams(
+            collective_id=collective_id, has_side_effects=True, vmem_limit_bytes=40 * 1024 * 1024
+        ),
+        name=f"combine_{collective_id}",
+    )(*operands)
+
+
+def round_up(value, unit):
+    return -(-value // unit) * unit
+
+
+def modes_gram_kernel(modes_ref, out_ref):
+    blocks = modes_ref.shape[1] // EDGE
+    at = 0
+    for i in range(blocks):
+        strip = product(modes_ref[:, i * EDGE : (i + 1) * EDGE], modes_ref[:, i * EDGE :], ((0,), (0,)))
+        for j in range(blocks - i):
+            out_ref[at : at + EDGE, :] = strip[:, j * EDGE : (j + 1) * EDGE]
+            at += EDGE
+    if at < out_ref.shape[0]:
+        out_ref[at:, :] = jnp.zeros((out_ref.shape[0] - at, EDGE), jnp.float32)
+
+
+def snapshot_gram_kernel(count, planes_ref, got_ref, modes_ref, rows_ref, out_ref):
+    held = got_ref.shape[0]
+    cells = lax.broadcasted_iota(jnp.int32, (EDGE, held), 1)
+    chosen = jnp.where(cells == planes_ref[...], 1.0, 0.0)
+    rows_ref[...] = product(chosen, got_ref[...])
+    snapshots = rows_ref[...]
+    blocks = modes_ref.shape[1] // EDGE
+    cross = product(snapshots[:count, :], modes_ref[...])
+    for i in range(blocks):
+        out_ref[i * count : (i + 1) * count, :] = cross[:, i * EDGE : (i + 1) * EDGE]
+    out_ref[blocks * count : (blocks + 1) * count, :] = product(snapshots[:count, :], snapshots, ((1,), (1,)))
+    at = (blocks + 1) * count
+    if at < out_ref.shape[0]:
+        out_ref[at:, :] = jnp.zeros((out_ref.shape[0] - at, EDGE), jnp.float32)
+
+
+def factor_kernel(count, rows_total, first_ref, second_ref, modes_ref, rows_ref, basis_ref, factor_ref,
+                  work, left, tile, upper, lower):
+    rank = modes_ref.shape[1]
+    size = rank + count
     whole = work.shape[0]
     blocks = whole // EDGE
-    work[...] = jnp.zeros_like(work)
-    work[:size, :size] = gram_ref[...]
-    tail = (blocks - 1) * EDGE
+    scale = 1.0 / rows_total
+    at = 0
+    for i in range(blocks - 1):
+        low = i * EDGE
+        for j in range(i, blocks - 1):
+            work[low : low + EDGE, j * EDGE : (j + 1) * EDGE] = first_ref[at : at + EDGE, :] * scale
+            at += EDGE
+        cross = jnp.concatenate(
+            [second_ref[i * count : (i + 1) * count, :], jnp.zeros((EDGE - count, EDGE), jnp.float32)], axis=0
+        )
+        work[low : low + EDGE, rank:] = cross.T * scale
     row = lax.broadcasted_iota(jnp.int32, (EDGE, EDGE), 0)
     col = lax.broadcasted_iota(jnp.int32, (EDGE, EDGE), 1)
-    padding = (row == col) & (row + tail >= size)
-    work[tail:, tail:] = jnp.where(padding, 1.0, work[tail:, tail:])
-    left[...] = jnp.zeros_like(left)
-    left[:, :size] = joined_ref[...]
+    inner = second_ref[(blocks - 1) * count : blocks * count, :] * scale
+    work[rank : rank + count, rank:] = inner
+    work[rank + count :, rank:] = jnp.where((row == col) & (row >= count), 1.0, 0.0)[count:, :]
+    left[:, :rank] = modes_ref[...]
+    left[:, rank:] = rows_ref[...].T
     factor_ref[...] = jnp.zeros_like(factor_ref)
 
     def step(k, carry):
@@ -141,54 +365,56 @@
     lax.fori_loop(0, blocks, step, 0)
 
 
-def factorize(gram, joined):
-    size = gram.shape[0]
-    rows = joined.shape[0]
-    whole = -(-size // EDGE) * EDGE
+def plain(kernel, out_shape, scratch, name, *operands):
     vmem = pl.BlockSpec(memory_space=pltpu.VMEM)
+    shapes = [jax.ShapeDtypeStruct(shape, jnp.float32) for shape in out_shape]
     return pl.pallas_call(
-        factor_kernel,
-        out_shape=(
-            jax.ShapeDtypeStruct((rows, size), jnp.float32),
-            jax.ShapeDtypeStruct((size, size), jnp.float32),
-        ),
-        in_specs=[vmem, vmem],
-        out_specs=(vmem, vmem),
-        scratch_shapes=[
-            pltpu.VMEM((whole, whole), jnp.float32),
-            pltpu.VMEM((rows, whole), jnp.float32),
-            pltpu.VMEM((EDGE, EDGE), jnp.float32),
-            pltpu.VMEM((EDGE, EDGE), jnp.float32),
-            pltpu.VMEM((EDGE, EDGE), jnp.float32),
-        ],
+        kernel,
+        out_shape=shapes,
+        in_specs=[vmem] * len(operands),
+        out_specs=[vmem] * len(shapes),
+        scratch_shapes=[pltpu.VMEM(shape, jnp.float32) for shape in scratch],
         compiler_params=pltpu.CompilerParams(vmem_limit_bytes=40 * 1024 * 1024),
-        name="factorize",
-    )(gram, joined)
-
-
-def on_device(velocity, modes, planes, assign):
+        name=name,
+    )(*operands)
+
+
+def decompose(advanced, modes, planes, assign):
     count = planes.shape[0]
     slabs = lax.axis_size("slab")
-    rows_total = modes.shape[0] * lax.axis_size("grp") * slabs * lax.axis_size("row")
+    devices = lax.axis_size("grp") * slabs * lax.axis_size("row")
+    rows, rank = modes.shape
+    size = rank + count
+    whole = rank + EDGE
+    depth = advanced.shape[1]
+    unit = PANEL * devices
+    blocks = rank // EDGE
+    (first,) = plain(modes_gram_kernel, [(round_up(blocks * (blocks + 1) // 2 * EDGE, unit), EDGE)], [],
+                     "modes_gram", modes)
+    pieces = jnp.transpose(advanced, (1, 0, 2, 3)).reshape(depth, slabs, -1)
+    mine = jnp.transpose(jnp.take(pieces, assign, axis=1, mode="clip"), (1, 0, 2))
+    first, got = combine(first, mine, 0)
+    chosen = jnp.pad(planes, (0, EDGE - count), constant_values=-1).reshape(EDGE, 1)
+    snapshots, second = plain(
+        functools.partial(snapshot_gram_kernel, count),
+        [(EDGE, rows), (round_up((blocks + 1) * count, unit), EDGE)], [], "snapshot_gram",
+        chosen, got.reshape(slabs * depth, rows), modes,
+    )
+    (second,) = combine(second, None, 1)
+    return plain(
+        functools.partial(factor_kernel, count, float(rows * devices)),
+        [(rows, size), (size, size)],
+        [(whole, whole), (rows, whole), (EDGE, EDGE), (EDGE, EDGE), (EDGE, EDGE)],
+        "factorize", first, second, modes, snapshots,
+    )
+
+
+def on_device(velocity, modes, planes, assign):
     first_q = step_size * tendency(velocity)
     middle = velocity + third * first_q
     second_q = carry_back * first_q + step_size * tendency(middle)
     advanced = middle + second_gain * second_q
-    depth = velocity.shape[1]
-    local_z = planes - lax.axis_index("slab") * depth
-    owned = (local_z >= 0) & (local_z < depth)
-    picked = jnp.take(advanced, jnp.clip(local_z, 0, depth - 1), axis=1)
-    picked = jnp.where(owned[None, :, None, None], picked, 0.0)
-    picked = jnp.transpose(picked, (1, 0, 2, 3)).reshape(count, slabs, -1)
-    arranged = jnp.take(picked, assign, axis=1)
-    received = lax.psum_scatter(
-        arranged.reshape(count, -1), "slab", scatter_dimension=1, tiled=True
-    )
-    snapshot_rows = received.T
-    joined = jnp.concatenate([modes, snapshot_rows], axis=1)
-    summed = lax.psum(product(joined.T, joined), ("grp", "slab", "row"))
-    gram = summed / float(rows_total)
-    basis, factor = factorize(gram, joined)
+    basis, factor = decompose(advanced, modes, planes, assign)
     return (advanced, basis, factor)
 
 

time: 264 us -> 140 us (0.53)
  waiting for transfers between devices: 177 us -> 18.2 us
  Pallas kernels: 26.6 us -> 85.5 us
  between operations: 14.3 us -> 0.88 us
  matrix products: 7.03 us -> 0 us
  other arithmetic: 8.91 us -> 5.44 us
    psum x1 -> x0, waiting for transfers between devices: 130 us -> none  [on_device(): summed = lax.psum(product(joined.T, joined), ('grp', 'slab', 'row'))]
    pallas_call x1 -> x5, Pallas kernels: 26.6 us -> 85.5 us  [the longest x2 54.9 us: combine(): pl.pallas_call(functools.partial(combine_kernel, chunks, swap), out_shape...]
    reduce_scatter x1 -> x0, waiting for transfers between devices: 26.4 us -> none  [on_device(): lax.psum_scatter(arranged.reshape(count, -1), 'slab', scatter_dimension=1...]
    dot_general x1 -> x0, matrix products: 7.03 us -> none  [product(): lax.dot_general(left, right, (dims, ((), ())), precision=lax.Precision.HI...]
    select_n x3 -> x0, other arithmetic: 2.68 us -> none  [the longest x2 2.48 us: on_device(): arranged = jnp.take(picked, assign, axis=1)]
  transfers between devices with their start and end apart: 14 -> 12, of which waited for: 7 -> 5; matrix products, arithmetic and copies ran while one was open for 2% -> 5% of each run, Pallas kernels for 0% -> 2%
where the time goes in v2:
time: 140 us; the launch traced here: 139 us
  Pallas kernels  85.5 us (61%)
  starting transfers between devices  18.7 us (13%)
  waiting for transfers between devices  18.2 us (13%)
  local copies, waits for them, and re-layouts  10.6 us (8%)
  other arithmetic  5.44 us (4%)
    pallas_call x2, Pallas kernels, combine(): pl.pallas_call(functools.partial(combine_kernel, chunks, swap), out_shape...  54.9 us
    pallas_call x3, Pallas kernels, plain(): pl.pallas_call(kernel, out_shape=shapes, in_specs=[vmem] * len(operands),...  30.6 us
    ppermute x6, starting transfers between devices, padded(): before = lax.ppermute(last, axis, up)  12.4 us
    ppermute x6, waiting for transfers between devices, padded(): after = lax.ppermute(initial, axis, down)  12.1 us
    ppermute x6, starting transfers between devices, padded(): after = lax.ppermute(initial, axis, down)  6.33 us
    ppermute x6, waiting for transfers between devices, padded(): before = lax.ppermute(last, axis, up)  6.13 us
    slice x4, local copies, waits for them, and re-layouts, padded(): last = lax.slice_in_dim(array, length - width, length, axis=dim)  4.41 us
    unnamed x20, local copies, waits for them, and re-layouts  3.27 us
  transfers between devices with their start and end apart: 12, of which 5 were waited for; matrix products, arithmetic and copies ran while one was open for 5% of the time, Pallas kernels for 2%

profile of v2, /device:TPU:0, one launch (start us, length us, event | category | flops | bytes accessed | tf_op | source)
XLA Modules:
  0.0 139.4 jit_solution(37206448163943850)
XLA Ops:
  0.6 2.0 %fusion.20 = (f32[3,32,2,128]{3,2,1,0:T(2,128)}, f32[3,32,2,128]{3,2,1,0:T(2,128)}) fusion(f32[3,32,8,128]{3,2,1,0:T(8,128)} %param.4), kind=kLoop, calls=%fused_computation.78 | loop fusion | bytes 393216 | tf_op jit(solution)/shard_map/slice | solution.py:24
  2.6 3.0 %collective-permute-start = (f32[3,32,2,128]{3,2,1,0:T(2,128)}, f32[3,32,2,128]{3,2,1,0:T(2,128)}, u32[]{:S(2)}, u32[]{:S(2)}) collective-permute-start(f32[3,32,2,128]{3,2,1,0:T(2,128)} %get-tuple-element.38), channel_id=1, source_target_pairs={{0,16},{16,0},{1,17},{17,1},{2,18},{18,2},{3,19},{19,3},{4,20},{20... | collective-permute-start | bytes 294920 | tf_op jit(solution)/shard_map/ppermute | solution.py:26
  5.7 2.2 %fusion.19 = (f32[3,32,8,2]{3,2,1,0:T(8,128)}, f32[3,32,8,2]{3,2,1,0:T(8,128)}) fusion(f32[3,32,8,128]{3,2,1,0:T(8,128)} %param.4), kind=kLoop, calls=%fused_computation.77 | loop fusion | bytes 24576 | tf_op jit(solution)/shard_map/slice | solution.py:24
  7.9 4.6 %collective-permute-start.2 = (f32[3,32,8,2]{3,2,1,0:T(8,128)}, f32[3,32,8,2]{3,2,1,0:T(8,128)}, u32[]{:S(2)}, u32[]{:S(2)}) collective-permute-start(f32[3,32,8,2]{3,2,1,0:T(8,128)} %get-tuple-element.36), channel_id=1, source_target_pairs={{0,1},{1,2},{2,3},{4,5},{5,6},{6,7},{8,9},{9,10},{10,11},{12,13},{... | collective-permute-start | bytes 18440 | tf_op jit(solution)/shard_map/ppermute | solution.py:26
  12.5 1.3 collective-permute-start.3
  15.6 2.3 %modes_gram.1.refs_0_ = f32[1280,128]{1,0:T(8,128)S(1)} custom-call(f32[768,512]{1,0:T(8,128)S(1)} %copy-done), custom_call_target="tpu_custom_call" | custom-call | tf_op jit(solution)/shard_map/modes_gram/pallas_call | solution.py:371
  17.9 6.9 %collective-permute-done.3 = f32[3,32,8,2]{3,2,1,0:T(8,128)} collective-permute-done((f32[3,32,8,2]{3,2,1,0:T(8,128)}, f32[3,32,8,2]{3,2,1,0:T(8,128)}, u32[]{:S(2)}, u32[]{:S(2)}) %collective-permute-start.3) | collective-permute-done | bytes 6176 | tf_op jit(solution)/shard_map/ppermute | solution.py:27
  24.8 1.0 constant_dynamic-update-slice_fusion.2
  26.7 1.7 %collective-permute-start.5 = (f32[3,2,12,128]{3,2,1,0:T(8,128)S(1)}, f32[3,2,12,128]{3,2,1,0:T(8,128)S(1)}, u32[]{:S(2)}, u32[]{:S(2)}) collective-permute-start(f32[3,2,12,128]{3,2,1,0:T(8,128)S(1)} %get-tuple-element.26), channel_id=1, source_target_pairs={{4,0},{8,4},{12,8},{0,12},{5,1},{9,5},{13,9},{1,13},{6,2},{10,6},{... | collective-permute-start | bytes 110600 | tf_op jit(solution)/shard_map/ppermute | solution.py:27
  28.4 0.9 constant_dynamic-update-slice_fusion
  30.2 2.5 %multiply_add_fusion = (f32[3,32,8,128]{3,2,1,0:T(8,128)S(1)}, f32[3,32,8,128]{3,2,1,0:T(8,128)S(1)}) fusion(f32[3,32,8,128]{3,2,1,0:T(8,128)S(1)} %copy-done.1, f32[32,8,128]{2,1,0:T(8,128)S(1)} %copy-done.6, f32[32,8,128]{2,1,0:T(8,128)S(1)} %copy-done.5, f32[32,8,128]{2,1,0:T(8,128)S(1)} %copy-done.4, f32[3,2,12,128]{3,2,1,0:T(8,128)S(1)} %collective-permute-done.5, ...), kind=kLoop, calls=%fused_computation.50 | loop fusion | flops 6291456 | bytes 3422208 | tf_op jit(solution)/shard_map/add | solution.py:414
  32.8 1.5 %collective-permute-start.6 = (f32[3,32,2,128]{3,2,1,0:T(2,128)S(1)}, f32[3,32,2,128]{3,2,1,0:T(2,128)S(1)}, u32[]{:S(2)}, u32[]{:S(2)}) collective-permute-start(f32[3,32,2,128]{3,2,1,0:T(2,128)S(1)} %get-tuple-element.32), channel_id=1, source_target_pairs={{0,16},{16,0},{1,17},{17,1},{2,18},{18,2},{3,19},{19,3},{4,20},{20... | collective-permute-start | bytes 294920 | tf_op jit(solution)/shard_map/ppermute | solution.py:26
  35.1 2.8 %collective-permute-start.8 = (f32[3,32,8,2]{3,2,1,0:T(8,128)S(1)}, f32[3,32,8,2]{3,2,1,0:T(8,128)S(1)}, u32[]{:S(2)}, u32[]{:S(2)}) collective-permute-start(f32[3,32,8,2]{3,2,1,0:T(8,128)S(1)} %get-tuple-element.30), channel_id=1, source_target_pairs={{0,1},{1,2},{2,3},{4,5},{5,6},{6,7},{8,9},{9,10},{10,11},{12,13},{... | collective-permute-start | bytes 18440 | tf_op jit(solution)/shard_map/ppermute | solution.py:26
  37.9 1.3 collective-permute-start.9
  39.2 0.9 collective-permute-done.7
  40.5 1.4 collective-permute-start.11
  41.9 5.3 %collective-permute-done.8 = f32[3,32,8,2]{3,2,1,0:T(8,128)S(1)} collective-permute-done((f32[3,32,8,2]{3,2,1,0:T(8,128)S(1)}, f32[3,32,8,2]{3,2,1,0:T(8,128)S(1)}, u32[]{:S(2)}, u32[]{:S(2)}) %collective-permute-start.8) | collective-permute-done | bytes 6176 | tf_op jit(solution)/shard_map/ppermute | solution.py:26
  47.2 4.3 %collective-permute-done.9 = f32[3,32,8,2]{3,2,1,0:T(8,128)S(1)} collective-permute-done((f32[3,32,8,2]{3,2,1,0:T(8,128)S(1)}, f32[3,32,8,2]{3,2,1,0:T(8,128)S(1)}, u32[]{:S(2)}, u32[]{:S(2)}) %collective-permute-start.9) | collective-permute-done | bytes 6176 | tf_op jit(solution)/shard_map/ppermute | solution.py:27
  51.5 1.3 fusion.9
  54.4 29.8 %combine_0.1 = (f32[1280,128]{1,0:T(8,128)S(1)}, f32[4,32,768]{2,1,0:T(8,128)S(1)}) custom-call(f32[1280,128]{1,0:T(8,128)S(1)} %modes_gram.1.refs_0_, f32[4,32,768]{2,1,0:T(8,128)S(1)} %gather_fusion), custom_call_target="tpu_custom_call" | custom-call | tf_op jit(solution)/shard_map/combine_0/pallas_call | solution.py:270
  84.2 1.8 %snapshot_gram.1 = (f32[128,768]{1,0:T(8,128)S(1)}, f32[512,128]{1,0:T(8,128)S(1)}) custom-call(s32[128,1]{1,0:T(8,128)S(1)} %copy.11.planes_ref, f32[128,768]{1,0:T(8,128)S(1)} %bitcast.18, f32[768,512]{1,0:T(8,128)S(1)} %copy-done), custom_call_target="tpu_custom_call" | custom-call | tf_op jit(solution)/shard_map/snapshot_gram/pallas_call | solution.py:371
  86.0 25.1 %combine_1.1.second_ref = f32[512,128]{1,0:T(8,128)S(1)} custom-call(f32[512,128]{1,0:T(8,128)S(1)} %get-tuple-element.11.refs_0_), custom_call_target="tpu_custom_call" | custom-call | tf_op jit(solution)/shard_map/combine_1/pallas_call | solution.py:270
  111.1 26.6 %factorize.1 = (f32[768,576]{1,0:T(8,128)S(1)}, f32[576,576]{1,0:T(8,128)}) custom-call(f32[1280,128]{1,0:T(8,128)S(1)} %get-tuple-element.9.first_ref, f32[512,128]{1,0:T(8,128)S(1)} %combine_1.1.second_ref, f32[768,512]{1,0:T(8,128)S(1)} %copy-done, f32[128,768]{1,0:T(8,128)S(1)} %get-tuple-element.12.rows_ref), custom_call_target="tpu_custom_call" | custom-call | tf_op jit(solution)/shard_map/factorize/pallas_call | solution.py:371
  137.7 1.7 %copy.12 = f32[768,576]{0,1:T(8,128)} copy(f32[768,576]{1,0:T(8,128)S(1)} %get-tuple-element.19) | data formatting | bytes 3538944
  (44 shorter events, 6.4 us)
Async XLA Ops:
  0.6 13.2 %copy-start.1 = (f32[3,32,8,128]{3,2,1,0:T(8,128)S(1)}, f32[3,32,8,128]{3,2,1,0:T(8,128)}, u32[]{:S(2)}) copy-start(f32[3,32,8,128]{3,2,1,0:T(8,128)} %param.4) | copy-start | bytes 1179652
  2.6 23.2 %collective-permute-start = (f32[3,32,2,128]{3,2,1,0:T(2,128)}, f32[3,32,2,128]{3,2,1,0:T(2,128)}, u32[]{:S(2)}, u32[]{:S(2)}) collective-permute-start(f32[3,32,2,128]{3,2,1,0:T(2,128)} %get-tuple-element.38), channel_id=1, source_target_pairs={{0,16},{16,0},{1,17},{17,1},{2,18},{18,2},{3,19},{19,3},{4,20},{20... | collective-permute-start | bytes 294920 | tf_op jit(solution)/shard_map/ppermute | solution.py:26
  5.6 9.8 %copy-start.7 = (s32[4]{0:T(128)S(1)}, s32[4]{0:T(128)}, u32[]{:S(2)}) copy-start(s32[4]{0:T(128)} %param.7) | copy-start | bytes 52
  5.6 9.8 %copy-start.8 = (s32[64]{0:T(128)S(1)}, s32[64]{0:T(128)}, u32[]{:S(2)}) copy-start(s32[64]{0:T(128)} %param.6) | copy-start | bytes 772
  5.6 9.9 %copy-start = (f32[768,512]{1,0:T(8,128)S(1)}, f32[768,512]{1,0:T(8,128)}, u32[]{:S(2)}) copy-start(f32[768,512]{1,0:T(8,128)} %modes_ref.5) | copy-start | bytes 4718596
  5.6 20.2 %collective-permute-start.1 = (f32[3,32,2,128]{3,2,1,0:T(2,128)}, f32[3,32,2,128]{3,2,1,0:T(2,128)}, u32[]{:S(2)}, u32[]{:S(2)}) collective-permute-start(f32[3,32,2,128]{3,2,1,0:T(2,128)} %get-tuple-element.39), channel_id=1, source_target_pairs={{16,0},{0,16},{17,1},{1,17},{18,2},{2,18},{19,3},{3,19},{20,4},{4,... | collective-permute-start | bytes 294920 | tf_op jit(solution)/shard_map/ppermute | solution.py:27
  7.9 21.5 %collective-permute-start.2 = (f32[3,32,8,2]{3,2,1,0:T(8,128)}, f32[3,32,8,2]{3,2,1,0:T(8,128)}, u32[]{:S(2)}, u32[]{:S(2)}) collective-permute-start(f32[3,32,8,2]{3,2,1,0:T(8,128)} %get-tuple-element.36), channel_id=1, source_target_pairs={{0,1},{1,2},{2,3},{4,5},{5,6},{6,7},{8,9},{9,10},{10,11},{12,13},{... | collective-permute-start | bytes 18440 | tf_op jit(solution)/shard_map/ppermute | solution.py:26
  12.5 12.3 %collective-permute-start.3 = (f32[3,32,8,2]{3,2,1,0:T(8,128)}, f32[3,32,8,2]{3,2,1,0:T(8,128)}, u32[]{:S(2)}, u32[]{:S(2)}) collective-permute-start(f32[3,32,8,2]{3,2,1,0:T(8,128)} %get-tuple-element.37), channel_id=1, source_target_pairs={{1,0},{2,1},{3,2},{5,4},{6,5},{7,6},{9,8},{10,9},{11,10},{13,12},{... | collective-permute-start | bytes 18440 | tf_op jit(solution)/shard_map/ppermute | solution.py:27
  15.5 9.2 %copy-start.2 = (f32[3,32,8,130]{3,2,1,0:T(8,128)S(1)}, f32[3,32,8,130]{3,2,1,0:T(8,128)}, u32[]{:S(2)}) copy-start(f32[3,32,8,130]{3,2,1,0:T(8,128)} %get-tuple-element.35) | copy-start | bytes 1198084
  15.5 14.6 %copy-start.4 = (f32[32,8,128]{2,1,0:T(8,128)S(1)}, f32[32,8,128]{2,1,0:T(8,128)}, u32[]{:S(2)}) copy-start(f32[32,8,128]{2,1,0:T(8,128)} %get-tuple-element.40) | copy-start | bytes 393220
  15.5 14.6 %copy-start.5 = (f32[32,8,128]{2,1,0:T(8,128)S(1)}, f32[32,8,128]{2,1,0:T(8,128)}, u32[]{:S(2)}) copy-start(f32[32,8,128]{2,1,0:T(8,128)} %get-tuple-element.41) | copy-start | bytes 393220
  15.6 14.6 %copy-start.6 = (f32[32,8,128]{2,1,0:T(8,128)S(1)}, f32[32,8,128]{2,1,0:T(8,128)}, u32[]{:S(2)}) copy-start(f32[32,8,128]{2,1,0:T(8,128)} %get-tuple-element.42) | copy-start | bytes 393220
  26.6 3.6 %collective-permute-start.4 = (f32[3,2,12,128]{3,2,1,0:T(8,128)S(1)}, f32[3,2,12,128]{3,2,1,0:T(8,128)S(1)}, u32[]{:S(2)}, u32[]{:S(2)}) collective-permute-start(f32[3,2,12,128]{3,2,1,0:T(8,128)S(1)} %get-tuple-element.25), channel_id=1, source_target_pairs={{0,4},{4,8},{8,12},{12,0},{1,5},{5,9},{9,13},{13,1},{2,6},{6,10},{... | collective-permute-start | bytes 110600 | tf_op jit(solution)/shard_map/ppermute | solution.py:26
  26.7 3.5 %collective-permute-start.5 = (f32[3,2,12,128]{3,2,1,0:T(8,128)S(1)}, f32[3,2,12,128]{3,2,1,0:T(8,128)S(1)}, u32[]{:S(2)}, u32[]{:S(2)}) collective-permute-start(f32[3,2,12,128]{3,2,1,0:T(8,128)S(1)} %get-tuple-element.26), channel_id=1, source_target_pairs={{4,0},{8,4},{12,8},{0,12},{5,1},{9,5},{13,9},{1,13},{6,2},{10,6},{... | collective-permute-start | bytes 110600 | tf_op jit(solution)/shard_map/ppermute | solution.py:27
  32.8 6.4 %collective-permute-start.6 = (f32[3,32,2,128]{3,2,1,0:T(2,128)S(1)}, f32[3,32,2,128]{3,2,1,0:T(2,128)S(1)}, u32[]{:S(2)}, u32[]{:S(2)}) collective-permute-start(f32[3,32,2,128]{3,2,1,0:T(2,128)S(1)} %get-tuple-element.32), channel_id=1, source_target_pairs={{0,16},{16,0},{1,17},{17,1},{2,18},{18,2},{3,19},{19,3},{4,20},{20... | collective-permute-start | bytes 294920 | tf_op jit(solution)/shard_map/ppermute | solution.py:26
  34.3 5.7 %collective-permute-start.7 = (f32[3,32,2,128]{3,2,1,0:T(2,128)S(1)}, f32[3,32,2,128]{3,2,1,0:T(2,128)S(1)}, u32[]{:S(2)}, u32[]{:S(2)}) collective-permute-start(f32[3,32,2,128]{3,2,1,0:T(2,128)S(1)} %get-tuple-element.33), channel_id=1, source_target_pairs={{16,0},{0,16},{17,1},{1,17},{18,2},{2,18},{19,3},{3,19},{20,4},{4,... | collective-permute-start | bytes 294920 | tf_op jit(solution)/shard_map/ppermute | solution.py:27
  35.1 12.2 %collective-permute-start.8 = (f32[3,32,8,2]{3,2,1,0:T(8,128)S(1)}, f32[3,32,8,2]{3,2,1,0:T(8,128)S(1)}, u32[]{:S(2)}, u32[]{:S(2)}) collective-permute-start(f32[3,32,8,2]{3,2,1,0:T(8,128)S(1)} %get-tuple-element.30), channel_id=1, source_target_pairs={{0,1},{1,2},{2,3},{4,5},{5,6},{6,7},{8,9},{9,10},{10,11},{12,13},{... | collective-permute-start | bytes 18440 | tf_op jit(solution)/shard_map/ppermute | solution.py:26
  37.9 13.7 %collective-permute-start.9 = (f32[3,32,8,2]{3,2,1,0:T(8,128)S(1)}, f32[3,32,8,2]{3,2,1,0:T(8,128)S(1)}, u32[]{:S(2)}, u32[]{:S(2)}) collective-permute-start(f32[3,32,8,2]{3,2,1,0:T(8,128)S(1)} %get-tuple-element.31), channel_id=1, source_target_pairs={{1,0},{2,1},{3,2},{5,4},{6,5},{7,6},{9,8},{10,9},{11,10},{13,12},{... | collective-permute-start | bytes 18440 | tf_op jit(solution)/shard_map/ppermute | solution.py:27
  40.1 11.4 %collective-permute-start.10 = (f32[3,2,12,128]{3,2,1,0:T(8,128)S(1)}, f32[3,2,12,128]{3,2,1,0:T(8,128)S(1)}, u32[]{:S(2)}, u32[]{:S(2)}) collective-permute-start(f32[3,2,12,128]{3,2,1,0:T(8,128)S(1)} %get-tuple-element.23), channel_id=1, source_target_pairs={{0,4},{4,8},{8,12},{12,0},{1,5},{5,9},{9,13},{13,1},{2,6},{6,10},{... | collective-permute-start | bytes 110600 | tf_op jit(solution)/shard_map/ppermute | solution.py:26
  40.5 11.0 %collective-permute-start.11 = (f32[3,2,12,128]{3,2,1,0:T(8,128)S(1)}, f32[3,2,12,128]{3,2,1,0:T(8,128)S(1)}, u32[]{:S(2)}, u32[]{:S(2)}) collective-permute-start(f32[3,2,12,128]{3,2,1,0:T(8,128)S(1)} %get-tuple-element.24), channel_id=1, source_target_pairs={{4,0},{8,4},{12,8},{0,12},{5,1},{9,5},{13,9},{1,13},{6,2},{10,6},{... | collective-permute-start | bytes 110600 | tf_op jit(solution)/shard_map/ppermute | solution.py:27
  52.8 0.7 copy-start.3

commit v3 on v2

--- a/solution.py
+++ b/solution.py
@@ -36,11 +36,12 @@
 
 
 def tendency(field):
-    wide = padded(field, (("grp", 2), ("slab", 1)), 2, True)
+    deep = padded(field, (("slab", 1),), 2, True)
+    wide = padded(field, (("grp", 2),), 2, True)
     walls = padded(field, (("row", 3),), 2, False)
     depth, across, height = (field.shape[1], field.shape[2], field.shape[3])
-    along_z = [wide[:, k : k + depth, 2 : 2 + across, :] for k in range(5)]
-    along_x = [wide[:, 2 : 2 + depth, k : k + across, :] for k in range(5)]
+    along_z = [deep[:, k : k + depth] for k in range(5)]
+    along_x = [wide[:, :, k : k + across, :] for k in range(5)]
     along_y = [walls[:, :, :, k : k + height] for k in range(5)]
     dz_first, dz_second = derivatives(along_z)
     dx_first, dx_second = derivatives(along_x)
@@ -100,23 +101,26 @@
 
 
 def wire_stages():
-    slabs = lax.axis_size("slab")
-    inner = 2 if slabs % 2 == 0 else 1
-    parts = [("slab", inner, slabs // inner), ("grp", 1, lax.axis_size("grp")), ("row", 1, lax.axis_size("row"))]
-    first = [("slab", 1, inner)]
-    return [first + parts[k:] + parts[:k] for k in range(3)]
+    slab = (("slab",), lax.axis_size("slab"))
+    rest = (("grp", "row"), lax.axis_size("grp") * lax.axis_size("row"))
+    return [[slab, rest], [rest, slab]]
 
 
 def place(stage):
-    axis, stride, members = stage
-    return lax.rem(lax.axis_index(axis) // stride, members)
+    index = 0
+    for axis in stage[0]:
+        index = index * lax.axis_size(axis) + lax.axis_index(axis)
+    return index
 
 
 def peer(stage, distance):
-    axis, stride, members = stage
-    mine = place(stage)
-    other = lax.rem(mine + distance, members)
-    return {axis: lax.axis_index(axis) + (other - mine) * stride}, other
+    axes, members = stage
+    other = lax.rem(place(stage) + distance, members)
+    coords, left = {}, other
+    for axis in reversed(axes):
+        coords[axis] = lax.rem(left, lax.axis_size(axis))
+        left = left // lax.axis_size(axis)
+    return coords, other
 
 
 def chunk_plan(rows, devices):
@@ -124,8 +128,8 @@
     units = rows // unit
     orders = wire_stages()
     chunks, base = [], 0
-    for c in range(3):
-        share = (units - sum(n for _, n, _ in chunks) + 2 - c) // (3 - c)
+    for c in range(2):
+        share = (units - base + 1 - c) // (2 - c)
         if share:
             chunks.append((base * unit, share, orders[c]))
             base += share
@@ -135,14 +139,14 @@
 def inbox_rows(chunks):
     total = 0
     for _, length, order in chunks:
-        for _, _, members in order:
+        for _, members in order:
             length //= members
             total += (members - 1) * length
     return total
 
 
 def wire_count(chunks):
-    return 2 * sum(members - 1 for _, _, order in chunks for _, _, members in order)
+    return 2 * sum(members - 1 for _, _, order in chunks for _, members in order)
 
 
 def combine_kernel(chunks, swap, *refs):
@@ -152,11 +156,10 @@
         part_ref, sum_ref, acc, full, inbox, send, recv = refs
     barrier = pltpu.get_barrier_semaphore()
     stages = chunks[0][2]
-    slab = ("slab", 1, lax.axis_size("slab"))
-    greeted = [slab] + [st for st in stages if st[0] != "slab"] if swap else stages
+    slab = (("slab",), lax.axis_size("slab"))
     total = 0
-    for stage in greeted:
-        for d in range(1, stage[2]):
+    for stage in stages:
+        for d in range(1, stage[1]):
             pl.semaphore_signal(barrier, inc=1, device_id=peer(stage, d)[0], device_id_type=pl.DeviceIdType.MESH)
             total += 1
     acc[...] = part_ref[...]
@@ -183,8 +186,8 @@
         started = []
         for c, (_, _, order) in enumerate(chunks):
             stage = order[s]
-            piece = lengths[c] // stage[2]
-            for d in range(1, stage[2]):
+            piece = lengths[c] // stage[1]
+            for d in range(1, stage[1]):
                 device, other = peer(stage, d)
                 source = acc.at[pl.ds(pl.multiple_of(offsets[c] + other * piece, PANEL), piece), :]
                 copy = begin(source, inbox.at[pl.ds(slot, piece), :], device, count)
@@ -193,7 +196,7 @@
                 slot += piece
         if swap and s == 0:
             me = lax.axis_index("slab")
-            for d in range(1, slab[2]):
+            for d in range(1, slab[1]):
                 device, other = peer(slab, d)
                 copy = pltpu.make_async_remote_copy(
                     src_ref=mine_ref.at[other], dst_ref=got.at[me],
@@ -204,7 +207,7 @@
                 swaps.append(copy)
         for c, (_, _, order) in enumerate(chunks):
             stage = order[s]
-            piece = lengths[c] // stage[2]
+            piece = lengths[c] // stage[1]
             trail[c].append((offsets[c], lengths[c]))
             offsets[c] = pl.multiple_of(offsets[c] + place(stage) * piece, PANEL)
             lengths[c] = piece
@@ -221,7 +224,7 @@
         for c, (_, _, order) in enumerate(chunks):
             stage = order[s]
             rows = pl.ds(offsets[c], lengths[c])
-            for d in range(1, stage[2]):
+            for d in range(1, stage[1]):
                 started.append(begin(full.at[rows, :], full.at[rows, :], peer(stage, d)[0], count))
                 count += 1
             offsets[c], lengths[c] = trail[c][s]
@@ -232,7 +235,7 @@
     if swap:
         for copy in swaps:
             copy.wait_recv()
-        for j in range(slab[2]):
+        for j in range(slab[1]):
             @pl.when(lax.axis_index("slab") == j)
             def _():
                 got_ref[j] = mine_ref[j]

time: 140 us -> 134 us (0.957)
  Pallas kernels: 85.5 us -> 78.1 us
  waiting for transfers between devices: 18.2 us -> 22.8 us
  other arithmetic: 5.44 us -> 3.32 us
    ppermute x6, waiting for transfers between devices: 12.1 us -> 20 us  [padded(): after = lax.ppermute(initial, axis, down)]
    pallas_call x2, Pallas kernels: 54.9 us -> 47.5 us  [combine(): pl.pallas_call(functools.partial(combine_kernel, chunks, swap), out_shape...]
    ppermute x6, waiting for transfers between devices: 6.13 us -> 2.77 us  [padded(): before = lax.ppermute(last, axis, up)]
    unnamed x20 -> x15, local copies, waits for them, and re-layouts: 3.27 us -> 2.58 us
    slice x4 -> x6, local copies, waits for them, and re-layouts: 4.41 us -> 5.1 us  [padded(): last = lax.slice_in_dim(array, length - width, length, axis=dim)]
  transfers between devices with their start and end apart: 12 -> 12, of which waited for: 5 -> 3; matrix products, arithmetic and copies ran while one was open for 5% -> 4% of each run, Pallas kernels for 2% -> 2%
where the time goes in v3:
time: 134 us; the launch traced here: 133 us
  Pallas kernels  78.1 us (58%)
  waiting for transfers between devices  22.8 us (17%)
  starting transfers between devices  18.6 us (14%)
  local copies, waits for them, and re-layouts  9.59 us (7%)
  other arithmetic  3.32 us (2%)
    pallas_call x2, Pallas kernels, combine(): pl.pallas_call(functools.partial(combine_kernel, chunks, swap), out_shape...  47.5 us
    pallas_call x3, Pallas kernels, plain(): pl.pallas_call(kernel, out_shape=shapes, in_specs=[vmem] * len(operands),...  30.6 us
    ppermute x6, waiting for transfers between devices, padded(): after = lax.ppermute(initial, axis, down)  20 us
    ppermute x6, starting transfers between devices, padded(): before = lax.ppermute(last, axis, up)  11.8 us
    ppermute x6, starting transfers between devices, padded(): after = lax.ppermute(initial, axis, down)  6.81 us
    slice x6, local copies, waits for them, and re-layouts, padded(): last = lax.slice_in_dim(array, length - width, length, axis=dim)  5.1 us
    ppermute x6, waiting for transfers between devices, padded(): before = lax.ppermute(last, axis, up)  2.77 us
  transfers between devices with their start and end apart: 12, of which 3 were waited for; matrix products, arithmetic and copies ran while one was open for 4% of the time, Pallas kernels for 2%

profile of v3, /device:TPU:0, one launch (start us, length us, event | category | flops | bytes accessed | tf_op | source)
XLA Modules:
  0.0 133.4 jit_solution(7566877183948848424)
XLA Ops:
  0.7 0.9 fusion.22
  2.0 2.0 %collective-permute-start.5 = (f32[3,2,8,128]{3,2,1,0:T(8,128)S(1)}, f32[3,2,8,128]{3,2,1,0:T(8,128)S(1)}, u32[]{:S(2)}, u32[]{:S(2)}) collective-permute-start(f32[3,2,8,128]{3,2,1,0:T(8,128)S(1)} %get-tuple-element.41), channel_id=1, source_target_pairs={{4,0},{8,4},{12,8},{0,12},{5,1},{9,5},{13,9},{1,13},{6,2},{10,6},{... | collective-permute-start | bytes 73736 | tf_op jit(solution)/shard_map/ppermute | solution.py:27
  4.0 1.9 %fusion.20 = (f32[3,32,2,128]{3,2,1,0:T(2,128)}, f32[3,32,2,128]{3,2,1,0:T(2,128)}) fusion(f32[3,32,8,128]{3,2,1,0:T(8,128)} %param.4), kind=kLoop, calls=%fused_computation.65 | loop fusion | bytes 393216 | tf_op jit(solution)/shard_map/slice | solution.py:24
  5.8 2.3 %collective-permute-start = (f32[3,32,2,128]{3,2,1,0:T(2,128)}, f32[3,32,2,128]{3,2,1,0:T(2,128)}, u32[]{:S(2)}, u32[]{:S(2)}) collective-permute-start(f32[3,32,2,128]{3,2,1,0:T(2,128)} %get-tuple-element.32), channel_id=1, source_target_pairs={{0,16},{16,0},{1,17},{17,1},{2,18},{18,2},{3,19},{19,3},{4,20},{20... | collective-permute-start | bytes 294920 | tf_op jit(solution)/shard_map/ppermute | solution.py:26
  8.2 2.1 %fusion.21 = (f32[3,32,8,2]{3,2,1,0:T(8,128)}, f32[3,32,8,2]{3,2,1,0:T(8,128)}) fusion(f32[3,32,8,128]{3,2,1,0:T(8,128)} %param.4), kind=kLoop, calls=%fused_computation.66 | loop fusion | bytes 24576 | tf_op jit(solution)/shard_map/slice | solution.py:24
  10.3 4.7 %collective-permute-start.2 = (f32[3,32,8,2]{3,2,1,0:T(8,128)}, f32[3,32,8,2]{3,2,1,0:T(8,128)}, u32[]{:S(2)}, u32[]{:S(2)}) collective-permute-start(f32[3,32,8,2]{3,2,1,0:T(8,128)} %get-tuple-element.38), channel_id=1, source_target_pairs={{0,1},{1,2},{2,3},{4,5},{5,6},{6,7},{8,9},{9,10},{10,11},{12,13},{... | collective-permute-start | bytes 18440 | tf_op jit(solution)/shard_map/ppermute | solution.py:26
  15.2 2.3 %modes_gram.1.refs_0_ = f32[1280,128]{1,0:T(8,128)S(1)} custom-call(f32[768,512]{1,0:T(8,128)S(1)} %copy-done), custom_call_target="tpu_custom_call" | custom-call | tf_op jit(solution)/shard_map/modes_gram/pallas_call | solution.py:374
  17.5 1.3 collective-permute-start.3
  19.0 10.5 %collective-permute-done.3 = f32[3,32,8,2]{3,2,1,0:T(8,128)S(1)} collective-permute-done((f32[3,32,8,2]{3,2,1,0:T(8,128)S(1)}, f32[3,32,8,2]{3,2,1,0:T(8,128)S(1)}, u32[]{:S(2)}, u32[]{:S(2)}) %collective-permute-start.3) | collective-permute-done | bytes 6176 | tf_op jit(solution)/shard_map/ppermute | solution.py:27
  29.5 0.9 constant_dynamic-update-slice_fusion
  30.5 2.1 %multiply_add_fusion = (f32[3,32,8,128]{3,2,1,0:T(8,128)S(1)}, f32[3,32,8,128]{3,2,1,0:T(8,128)S(1)}) fusion(f32[3,32,8,128]{3,2,1,0:T(8,128)S(1)} %copy-done.1, f32[32,8,128]{2,1,0:T(8,128)S(1)} %get-tuple-element.44, f32[32,8,128]{2,1,0:T(8,128)S(1)} %get-tuple-element.43, f32[32,8,128]{2,1,0:T(8,128)S(1)} %get-tuple-element.42, ...), kind=kLoop, calls=%fused_computation.42 | loop fusion | flops 5111808 | bytes 4823040 | tf_op jit(solution)/shard_map/add | solution.py:417
  32.9 2.8 %collective-permute-start.8 = (f32[3,32,8,2]{3,2,1,0:T(8,128)S(1)}, f32[3,32,8,2]{3,2,1,0:T(8,128)S(1)}, u32[]{:S(2)}, u32[]{:S(2)}) collective-permute-start(f32[3,32,8,2]{3,2,1,0:T(8,128)S(1)} %get-tuple-element.28), channel_id=1, source_target_pairs={{0,1},{1,2},{2,3},{4,5},{5,6},{6,7},{8,9},{9,10},{10,11},{12,13},{... | collective-permute-start | bytes 18440 | tf_op jit(solution)/shard_map/ppermute | solution.py:26
  35.7 1.7 %collective-permute-start.11 = (f32[3,2,8,128]{3,2,1,0:T(8,128)S(1)}, f32[3,2,8,128]{3,2,1,0:T(8,128)S(1)}, u32[]{:S(2)}, u32[]{:S(2)}) collective-permute-start(f32[3,2,8,128]{3,2,1,0:T(8,128)S(1)} %get-tuple-element.31), channel_id=1, source_target_pairs={{4,0},{8,4},{12,8},{0,12},{5,1},{9,5},{13,9},{1,13},{6,2},{10,6},{... | collective-permute-start | bytes 73736 | tf_op jit(solution)/shard_map/ppermute | solution.py:27
  37.5 1.5 %collective-permute-start.6 = (f32[3,32,2,128]{3,2,1,0:T(2,128)S(1)}, f32[3,32,2,128]{3,2,1,0:T(2,128)S(1)}, u32[]{:S(2)}, u32[]{:S(2)}) collective-permute-start(f32[3,32,2,128]{3,2,1,0:T(2,128)S(1)} %get-tuple-element.26), channel_id=1, source_target_pairs={{0,16},{16,0},{1,17},{17,1},{2,18},{18,2},{3,19},{19,3},{4,20},{20... | collective-permute-start | bytes 294920 | tf_op jit(solution)/shard_map/ppermute | solution.py:26
  39.5 2.8 %collective-permute-done.8 = f32[3,32,8,2]{3,2,1,0:T(8,128)S(1)} collective-permute-done((f32[3,32,8,2]{3,2,1,0:T(8,128)S(1)}, f32[3,32,8,2]{3,2,1,0:T(8,128)S(1)}, u32[]{:S(2)}, u32[]{:S(2)}) %collective-permute-start.8) | collective-permute-done | bytes 6176 | tf_op jit(solution)/shard_map/ppermute | solution.py:26
  42.2 1.3 collective-permute-start.9
  43.6 9.5 %collective-permute-done.9 = f32[3,32,8,2]{3,2,1,0:T(8,128)S(1)} collective-permute-done((f32[3,32,8,2]{3,2,1,0:T(8,128)S(1)}, f32[3,32,8,2]{3,2,1,0:T(8,128)S(1)}, u32[]{:S(2)}, u32[]{:S(2)}) %collective-permute-start.9) | collective-permute-done | bytes 6176 | tf_op jit(solution)/shard_map/ppermute | solution.py:27
  53.1 1.1 fusion.11
  54.2 0.7 copy-done.2
  55.8 25.6 %combine_0.1 = (f32[1280,128]{1,0:T(8,128)S(1)}, f32[4,32,768]{2,1,0:T(8,128)S(1)}) custom-call(f32[1280,128]{1,0:T(8,128)S(1)} %modes_gram.1.refs_0_, f32[4,32,768]{2,1,0:T(8,128)S(1)} %gather_fusion), custom_call_target="tpu_custom_call" | custom-call | tf_op jit(solution)/shard_map/combine_0/pallas_call | solution.py:273
  81.5 1.8 %snapshot_gram.1 = (f32[128,768]{1,0:T(8,128)S(1)}, f32[512,128]{1,0:T(8,128)S(1)}) custom-call(s32[128,1]{1,0:T(8,128)S(1)} %copy.11.planes_ref, f32[128,768]{1,0:T(8,128)S(1)} %bitcast.18, f32[768,512]{1,0:T(8,128)S(1)} %copy-done), custom_call_target="tpu_custom_call" | custom-call | tf_op jit(solution)/shard_map/snapshot_gram/pallas_call | solution.py:374
  83.2 21.9 %combine_1.1.second_ref = f32[512,128]{1,0:T(8,128)S(1)} custom-call(f32[512,128]{1,0:T(8,128)S(1)} %get-tuple-element.11.refs_0_), custom_call_target="tpu_custom_call" | custom-call | tf_op jit(solution)/shard_map/combine_1/pallas_call | solution.py:273
  105.1 26.6 %factorize.1 = (f32[768,576]{1,0:T(8,128)S(1)}, f32[576,576]{1,0:T(8,128)}) custom-call(f32[1280,128]{1,0:T(8,128)S(1)} %get-tuple-element.9.first_ref, f32[512,128]{1,0:T(8,128)S(1)} %combine_1.1.second_ref, f32[768,512]{1,0:T(8,128)S(1)} %copy-done, f32[128,768]{1,0:T(8,128)S(1)} %get-tuple-element.12.rows_ref), custom_call_target="tpu_custom_call" | custom-call | tf_op jit(solution)/shard_map/factorize/pallas_call | solution.py:374
  131.7 1.7 %copy.12 = f32[768,576]{0,1:T(8,128)} copy(f32[768,576]{1,0:T(8,128)S(1)} %get-tuple-element.19) | data formatting | bytes 3538944
  (40 shorter events, 2.5 us)
Async XLA Ops:
  0.6 14.4 %copy-start.1 = (f32[3,32,8,128]{3,2,1,0:T(8,128)S(1)}, f32[3,32,8,128]{3,2,1,0:T(8,128)}, u32[]{:S(2)}) copy-start(f32[3,32,8,128]{3,2,1,0:T(8,128)} %param.4) | copy-start | bytes 1179652
  0.6 14.4 %copy-start.4 = (s32[4]{0:T(128)S(1)}, s32[4]{0:T(128)}, u32[]{:S(2)}) copy-start(s32[4]{0:T(128)} %param.7) | copy-start | bytes 52
  0.7 14.4 %copy-start.5 = (s32[64]{0:T(128)S(1)}, s32[64]{0:T(128)}, u32[]{:S(2)}) copy-start(s32[64]{0:T(128)} %param.6) | copy-start | bytes 772
  0.7 14.5 %copy-start = (f32[768,512]{1,0:T(8,128)S(1)}, f32[768,512]{1,0:T(8,128)}, u32[]{:S(2)}) copy-start(f32[768,512]{1,0:T(8,128)} %modes_ref.5) | copy-start | bytes 4718596
  1.6 16.0 %collective-permute-start.4 = (f32[3,2,8,128]{3,2,1,0:T(8,128)S(1)}, f32[3,2,8,128]{3,2,1,0:T(8,128)S(1)}, u32[]{:S(2)}, u32[]{:S(2)}) collective-permute-start(f32[3,2,8,128]{3,2,1,0:T(8,128)S(1)} %get-tuple-element.40), channel_id=1, source_target_pairs={{0,4},{4,8},{8,12},{12,0},{1,5},{5,9},{9,13},{13,1},{2,6},{6,10},{... | collective-permute-start | bytes 73736 | tf_op jit(solution)/shard_map/ppermute | solution.py:26
  2.0 27.5 %collective-permute-start.5 = (f32[3,2,8,128]{3,2,1,0:T(8,128)S(1)}, f32[3,2,8,128]{3,2,1,0:T(8,128)S(1)}, u32[]{:S(2)}, u32[]{:S(2)}) collective-permute-start(f32[3,2,8,128]{3,2,1,0:T(8,128)S(1)} %get-tuple-element.41), channel_id=1, source_target_pairs={{4,0},{8,4},{12,8},{0,12},{5,1},{9,5},{13,9},{1,13},{6,2},{10,6},{... | collective-permute-start | bytes 73736 | tf_op jit(solution)/shard_map/ppermute | solution.py:27
  5.8 24.7 %collective-permute-start = (f32[3,32,2,128]{3,2,1,0:T(2,128)}, f32[3,32,2,128]{3,2,1,0:T(2,128)}, u32[]{:S(2)}, u32[]{:S(2)}) collective-permute-start(f32[3,32,2,128]{3,2,1,0:T(2,128)} %get-tuple-element.32), channel_id=1, source_target_pairs={{0,16},{16,0},{1,17},{17,1},{2,18},{18,2},{3,19},{19,3},{4,20},{20... | collective-permute-start | bytes 294920 | tf_op jit(solution)/shard_map/ppermute | solution.py:26
  8.1 21.4 %collective-permute-start.1 = (f32[3,32,2,128]{3,2,1,0:T(2,128)}, f32[3,32,2,128]{3,2,1,0:T(2,128)}, u32[]{:S(2)}, u32[]{:S(2)}) collective-permute-start(f32[3,32,2,128]{3,2,1,0:T(2,128)} %get-tuple-element.33), channel_id=1, source_target_pairs={{16,0},{0,16},{17,1},{1,17},{18,2},{2,18},{19,3},{3,19},{20,4},{4,... | collective-permute-start | bytes 294920 | tf_op jit(solution)/shard_map/ppermute | solution.py:27
  10.3 20.2 %collective-permute-start.2 = (f32[3,32,8,2]{3,2,1,0:T(8,128)}, f32[3,32,8,2]{3,2,1,0:T(8,128)}, u32[]{:S(2)}, u32[]{:S(2)}) collective-permute-start(f32[3,32,8,2]{3,2,1,0:T(8,128)} %get-tuple-element.38), channel_id=1, source_target_pairs={{0,1},{1,2},{2,3},{4,5},{5,6},{6,7},{8,9},{9,10},{10,11},{12,13},{... | collective-permute-start | bytes 18440 | tf_op jit(solution)/shard_map/ppermute | solution.py:26
  15.2 2.3 %copy-start.3 = (f32[3,32,8,2]{3,2,1,0:T(8,128)S(1)}, f32[3,32,8,2]{3,2,1,0:T(8,128)}, u32[]{:S(2)}) copy-start(f32[3,32,8,2]{3,2,1,0:T(8,128)} %get-tuple-element.39) | copy-start | bytes 18436
  17.5 11.9 %collective-permute-start.3 = (f32[3,32,8,2]{3,2,1,0:T(8,128)S(1)}, f32[3,32,8,2]{3,2,1,0:T(8,128)S(1)}, u32[]{:S(2)}, u32[]{:S(2)}) collective-permute-start(f32[3,32,8,2]{3,2,1,0:T(8,128)S(1)} %copy-done.3), channel_id=1, source_target_pairs={{1,0},{2,1},{3,2},{5,4},{6,5},{7,6},{9,8},{10,9},{11,10},{13,12},{... | collective-permute-start | bytes 18440 | tf_op jit(solution)/shard_map/ppermute | solution.py:27
  32.9 9.4 %collective-permute-start.8 = (f32[3,32,8,2]{3,2,1,0:T(8,128)S(1)}, f32[3,32,8,2]{3,2,1,0:T(8,128)S(1)}, u32[]{:S(2)}, u32[]{:S(2)}) collective-permute-start(f32[3,32,8,2]{3,2,1,0:T(8,128)S(1)} %get-tuple-element.28), channel_id=1, source_target_pairs={{0,1},{1,2},{2,3},{4,5},{5,6},{6,7},{8,9},{9,10},{10,11},{12,13},{... | collective-permute-start | bytes 18440 | tf_op jit(solution)/shard_map/ppermute | solution.py:26
  35.7 17.4 %collective-permute-start.10 = (f32[3,2,8,128]{3,2,1,0:T(8,128)S(1)}, f32[3,2,8,128]{3,2,1,0:T(8,128)S(1)}, u32[]{:S(2)}, u32[]{:S(2)}) collective-permute-start(f32[3,2,8,128]{3,2,1,0:T(8,128)S(1)} %get-tuple-element.30), channel_id=1, source_target_pairs={{0,4},{4,8},{8,12},{12,0},{1,5},{5,9},{9,13},{13,1},{2,6},{6,10},{... | collective-permute-start | bytes 73736 | tf_op jit(solution)/shard_map/ppermute | solution.py:26
  35.7 17.4 %collective-permute-start.11 = (f32[3,2,8,128]{3,2,1,0:T(8,128)S(1)}, f32[3,2,8,128]{3,2,1,0:T(8,128)S(1)}, u32[]{:S(2)}, u32[]{:S(2)}) collective-permute-start(f32[3,2,8,128]{3,2,1,0:T(8,128)S(1)} %get-tuple-element.31), channel_id=1, source_target_pairs={{4,0},{8,4},{12,8},{0,12},{5,1},{9,5},{13,9},{1,13},{6,2},{10,6},{... | collective-permute-start | bytes 73736 | tf_op jit(solution)/shard_map/ppermute | solution.py:27
  37.5 15.6 %collective-permute-start.6 = (f32[3,32,2,128]{3,2,1,0:T(2,128)S(1)}, f32[3,32,2,128]{3,2,1,0:T(2,128)S(1)}, u32[]{:S(2)}, u32[]{:S(2)}) collective-permute-start(f32[3,32,2,128]{3,2,1,0:T(2,128)S(1)} %get-tuple-element.26), channel_id=1, source_target_pairs={{0,16},{16,0},{1,17},{17,1},{2,18},{18,2},{3,19},{19,3},{4,20},{20... | collective-permute-start | bytes 294920 | tf_op jit(solution)/shard_map/ppermute | solution.py:26
  39.0 14.1 %collective-permute-start.7 = (f32[3,32,2,128]{3,2,1,0:T(2,128)S(1)}, f32[3,32,2,128]{3,2,1,0:T(2,128)S(1)}, u32[]{:S(2)}, u32[]{:S(2)}) collective-permute-start(f32[3,32,2,128]{3,2,1,0:T(2,128)S(1)} %get-tuple-element.27), channel_id=1, source_target_pairs={{16,0},{0,16},{17,1},{1,17},{18,2},{2,18},{19,3},{3,19},{20,4},{4,... | collective-permute-start | bytes 294920 | tf_op jit(solution)/shard_map/ppermute | solution.py:27
  42.2 10.8 %collective-permute-start.9 = (f32[3,32,8,2]{3,2,1,0:T(8,128)S(1)}, f32[3,32,8,2]{3,2,1,0:T(8,128)S(1)}, u32[]{:S(2)}, u32[]{:S(2)}) collective-permute-start(f32[3,32,8,2]{3,2,1,0:T(8,128)S(1)} %get-tuple-element.29), channel_id=1, source_target_pairs={{1,0},{2,1},{3,2},{5,4},{6,5},{7,6},{9,8},{10,9},{11,10},{13,12},{... | collective-permute-start | bytes 18440 | tf_op jit(solution)/shard_map/ppermute | solution.py:27
  54.2 0.7 copy-start.2

commit v4 on v3

--- a/solution.py
+++ b/solution.py
@@ -123,7 +123,7 @@
     return coords, other
 
 
-def chunk_plan(rows, devices):
+def chunk_plan(origin, rows, devices):
     unit = PANEL * devices
     units = rows // unit
     orders = wire_stages()
@@ -133,7 +133,7 @@
         if share:
             chunks.append((base * unit, share, orders[c]))
             base += share
-    return [(start, share * unit, order) for start, share, order in chunks]
+    return [(origin + start, share * unit, order) for start, share, order in chunks]
 
 
 def inbox_rows(chunks):
@@ -149,31 +149,37 @@
     return 2 * sum(members - 1 for _, _, order in chunks for _, members in order)
 
 
-def combine_kernel(chunks, swap, *refs):
-    if swap:
-        part_ref, mine_ref, sum_ref, got_ref, acc, full, inbox, send, recv, got, swap_send, swap_recv = refs
-    else:
-        part_ref, sum_ref, acc, full, inbox, send, recv = refs
+def combine_kernel(chunks, early, count, *refs):
+    (part_ref, mine_ref, modes_ref, planes_ref, first_ref, second_ref, rows_ref,
+     acc, full, inbox, send, recv, got, swap_send, swap_recv) = refs
     barrier = pltpu.get_barrier_semaphore()
     stages = chunks[0][2]
+    deep = len(stages)
     slab = (("slab",), lax.axis_size("slab"))
     total = 0
     for stage in stages:
         for d in range(1, stage[1]):
             pl.semaphore_signal(barrier, inc=1, device_id=peer(stage, d)[0], device_id_type=pl.DeviceIdType.MESH)
             total += 1
-    acc[...] = part_ref[...]
+    head = part_ref.shape[0]
+    acc[:head, :] = part_ref[...]
+    me = lax.axis_index("slab")
+    for j in range(slab[1]):
+        @pl.when(me == j)
+        def _():
+            got[j] = mine_ref[j]
+
     pl.semaphore_wait(barrier, total)
 
-    count = 0
-    slot = 0
+    used = [0, 0]
     pending = []
 
-    def begin(source, target, device, index):
+    def begin(source, target, device):
         copy = pltpu.make_async_remote_copy(
-            src_ref=source, dst_ref=target, send_sem=send.at[index], recv_sem=recv.at[index],
+            src_ref=source, dst_ref=target, send_sem=send.at[used[0]], recv_sem=recv.at[used[0]],
             device_id=device, device_id_type=pl.DeviceIdType.MESH,
         )
+        used[0] += 1
         copy.start()
         pending.append(copy)
         return copy
@@ -181,106 +187,97 @@
     offsets = [jnp.int32(base) for base, _, _ in chunks]
     lengths = [length for _, length, _ in chunks]
     trail = [[] for _ in chunks]
-    swaps = []
-    for s in range(len(stages)):
+
+    def launch(c, phase):
         started = []
-        for c, (_, _, order) in enumerate(chunks):
-            stage = order[s]
+        if phase < deep:
+            stage = chunks[c][2][phase]
             piece = lengths[c] // stage[1]
             for d in range(1, stage[1]):
                 device, other = peer(stage, d)
                 source = acc.at[pl.ds(pl.multiple_of(offsets[c] + other * piece, PANEL), piece), :]
-                copy = begin(source, inbox.at[pl.ds(slot, piece), :], device, count)
-                started.append((c, copy, slot, piece))
-                count += 1
-                slot += piece
-        if swap and s == 0:
-            me = lax.axis_index("slab")
-            for d in range(1, slab[1]):
-                device, other = peer(slab, d)
-                copy = pltpu.make_async_remote_copy(
-                    src_ref=mine_ref.at[other], dst_ref=got.at[me],
-                    send_sem=swap_send.at[d - 1], recv_sem=swap_recv.at[d - 1],
-                    device_id=device, device_id_type=pl.DeviceIdType.MESH,
-                )
-                copy.start()
-                swaps.append(copy)
-        for c, (_, _, order) in enumerate(chunks):
-            stage = order[s]
-            piece = lengths[c] // stage[1]
+                slot = used[1]
+                started.append((begin(source, inbox.at[pl.ds(slot, piece), :], device), slot))
+                used[1] += piece
             trail[c].append((offsets[c], lengths[c]))
             offsets[c] = pl.multiple_of(offsets[c] + place(stage) * piece, PANEL)
             lengths[c] = piece
-            rows = pl.ds(offsets[c], piece)
-            for owner, copy, where, size in started:
-                if owner == c:
-                    copy.wait_recv()
-                    acc[rows, :] = acc[rows, :] + inbox[pl.ds(where, size), :]
-    for c in range(len(chunks)):
+        else:
+            stage = chunks[c][2][2 * deep - 1 - phase]
+            rows = pl.ds(offsets[c], lengths[c])
+            if phase == deep:
+                full[rows, :] = acc[rows, :]
+            for d in range(1, stage[1]):
+                started.append((begin(full.at[rows, :], full.at[rows, :], peer(stage, d)[0]), 0))
+            offsets[c], lengths[c] = trail[c][2 * deep - 1 - phase]
+            offsets[c] = pl.multiple_of(offsets[c], PANEL)
+        return started
+
+    def finish(c, phase, started):
         rows = pl.ds(offsets[c], lengths[c])
-        full[rows, :] = acc[rows, :]
-    for s in reversed(range(len(stages))):
-        started = []
-        for c, (_, _, order) in enumerate(chunks):
-            stage = order[s]
-            rows = pl.ds(offsets[c], lengths[c])
-            for d in range(1, stage[1]):
-                started.append(begin(full.at[rows, :], full.at[rows, :], peer(stage, d)[0], count))
-                count += 1
-            offsets[c], lengths[c] = trail[c][s]
-            offsets[c] = pl.multiple_of(offsets[c], PANEL)
-        for copy in started:
+        for copy, slot in started:
             copy.wait_recv()
-    sum_ref[...] = full[...]
-    if swap:
-        for copy in swaps:
-            copy.wait_recv()
-        for j in range(slab[1]):
-            @pl.when(lax.axis_index("slab") == j)
-            def _():
-                got_ref[j] = mine_ref[j]
-
-            @pl.when(lax.axis_index("slab") != j)
-            def _():
-                got_ref[j] = got[j]
+            if phase < deep:
+                acc[rows, :] = acc[rows, :] + inbox[pl.ds(slot, lengths[c]), :]
+
+    swaps = []
+    for d in range(1, slab[1]):
+        device, other = peer(slab, d)
+        copy = pltpu.make_async_remote_copy(
+            src_ref=mine_ref.at[other], dst_ref=got.at[me],
+            send_sem=swap_send.at[d - 1], recv_sem=swap_recv.at[d - 1],
+            device_id=device, device_id_type=pl.DeviceIdType.MESH,
+        )
+        copy.start()
+        swaps.append(copy)
+    late = range(early, len(chunks))
+    for tick in range(2 * deep + 1):
+        active = []
+        if tick < 2 * deep:
+            active += [(c, tick, launch(c, tick)) for c in range(early)]
+        if tick == 1:
+            for copy in swaps:
+                copy.wait_recv()
+            snapshot_gram(count, planes_ref, got, modes_ref, rows_ref, acc, head)
+        if tick >= 1:
+            active += [(c, tick - 1, launch(c, tick - 1)) for c in late]
+        for c, phase, started in active:
+            finish(c, phase, started)
+    first_ref[...] = full[:head, :]
+    second_ref[...] = full[head:, :]
     for copy in pending + swaps:
         copy.wait_send()
 
 
-def combine(part, mine, collective_id):
+def combine(part, mine, modes, chosen, count):
     devices = lax.axis_size("grp") * lax.axis_size("slab") * lax.axis_size("row")
-    chunks = chunk_plan(part.shape[0], devices)
-    swap = mine is not None
+    head = part.shape[0]
+    extra = round_up((modes.shape[1] // EDGE + 1) * count, PANEL * devices)
+    first = chunk_plan(0, head, devices)
+    chunks = first + chunk_plan(head, extra, devices)
     wires = wire_count(chunks)
     vmem = pl.BlockSpec(memory_space=pltpu.VMEM)
-    out = [jax.ShapeDtypeStruct(part.shape, jnp.float32)]
-    scratch = [
-        pltpu.VMEM(part.shape, jnp.float32),
-        pltpu.VMEM(part.shape, jnp.float32),
-        pltpu.VMEM((inbox_rows(chunks), EDGE), jnp.float32),
-        pltpu.SemaphoreType.DMA((wires,)),
-        pltpu.SemaphoreType.DMA((wires,)),
-    ]
-    operands = [part]
-    if swap:
-        operands.append(mine)
-        out.append(jax.ShapeDtypeStruct(mine.shape, jnp.float32))
-        scratch += [
+    shapes = [(head, EDGE), (extra, EDGE), (EDGE, modes.shape[0])]
+    return pl.pallas_call(
+        functools.partial(combine_kernel, chunks, len(first), count),
+        out_shape=[jax.ShapeDtypeStruct(shape, jnp.float32) for shape in shapes],
+        in_specs=[vmem] * 4,
+        out_specs=[vmem] * 3,
+        scratch_shapes=[
+            pltpu.VMEM((head + extra, EDGE), jnp.float32),
+            pltpu.VMEM((head + extra, EDGE), jnp.float32),
+            pltpu.VMEM((inbox_rows(chunks), EDGE), jnp.float32),
+            pltpu.SemaphoreType.DMA((wires,)),
+            pltpu.SemaphoreType.DMA((wires,)),
             pltpu.VMEM(mine.shape, jnp.float32),
             pltpu.SemaphoreType.DMA((mine.shape[0] - 1,)),
             pltpu.SemaphoreType.DMA((mine.shape[0] - 1,)),
-        ]
-    return pl.pallas_call(
-        functools.partial(combine_kernel, chunks, swap),
-        out_shape=out,
-        in_specs=[vmem] * len(operands),
-        out_specs=[vmem] * len(out),
-        scratch_shapes=scratch,
+        ],
         compiler_params=pltpu.CompilerParams(
-            collective_id=collective_id, has_side_effects=True, vmem_limit_bytes=40 * 1024 * 1024
+            collective_id=0, has_side_effects=True, vmem_limit_bytes=48 * 1024 * 1024
         ),
-        name=f"combine_{collective_id}",
-    )(*operands)
+        name="combine",
+    )(part, mine, modes, chosen)
 
 
 def round_up(value, unit):
@@ -299,18 +296,20 @@
         out_ref[at:, :] = jnp.zeros((out_ref.shape[0] - at, EDGE), jnp.float32)
 
 
-def snapshot_gram_kernel(count, planes_ref, got_ref, modes_ref, rows_ref, out_ref):
-    held = got_ref.shape[0]
-    cells = lax.broadcasted_iota(jnp.int32, (EDGE, held), 1)
+def snapshot_gram(count, planes_ref, got_ref, modes_ref, rows_ref, out_ref, base):
+    slabs, depth = got_ref.shape[0], got_ref.shape[1]
+    cells = lax.broadcasted_iota(jnp.int32, (EDGE, slabs * depth), 1)
     chosen = jnp.where(cells == planes_ref[...], 1.0, 0.0)
-    rows_ref[...] = product(chosen, got_ref[...])
-    snapshots = rows_ref[...]
+    held = got_ref[...].reshape(slabs * depth, got_ref.shape[2])
+    snapshots = product(chosen, held)
+    rows_ref[...] = snapshots
     blocks = modes_ref.shape[1] // EDGE
     cross = product(snapshots[:count, :], modes_ref[...])
     for i in range(blocks):
-        out_ref[i * count : (i + 1) * count, :] = cross[:, i * EDGE : (i + 1) * EDGE]
-    out_ref[blocks * count : (blocks + 1) * count, :] = product(snapshots[:count, :], snapshots, ((1,), (1,)))
-    at = (blocks + 1) * count
+        out_ref[base + i * count : base + (i + 1) * count, :] = cross[:, i * EDGE : (i + 1) * EDGE]
+    at = base + blocks * count
+    out_ref[at : at + count, :] = product(snapshots[:count, :], snapshots, ((1,), (1,)))
+    at += count
     if at < out_ref.shape[0]:
         out_ref[at:, :] = jnp.zeros((out_ref.shape[0] - at, EDGE), jnp.float32)
 
@@ -396,14 +395,8 @@
                      "modes_gram", modes)
     pieces = jnp.transpose(advanced, (1, 0, 2, 3)).reshape(depth, slabs, -1)
     mine = jnp.transpose(jnp.take(pieces, assign, axis=1, mode="clip"), (1, 0, 2))
-    first, got = combine(first, mine, 0)
     chosen = jnp.pad(planes, (0, EDGE - count), constant_values=-1).reshape(EDGE, 1)
-    snapshots, second = plain(
-        functools.partial(snapshot_gram_kernel, count),
-        [(EDGE, rows), (round_up((blocks + 1) * count, unit), EDGE)], [], "snapshot_gram",
-        chosen, got.reshape(slabs * depth, rows), modes,
-    )
-    (second,) = combine(second, None, 1)
+    first, second, snapshots = combine(first, mine, modes, chosen, count)
     return plain(
         functools.partial(factor_kernel, count, float(rows * devices)),
         [(rows, size), (size, size)],

time: 134 us -> 123 us (0.918)
  Pallas kernels: 78.1 us -> 67.1 us
    pallas_call x2 -> x1, Pallas kernels: 47.5 us -> 38.2 us  [combine(): pl.pallas_call(functools.partial(combine_kernel, chunks, len(first), coun...]
    pallas_call x3 -> x2, Pallas kernels: 30.6 us -> 28.9 us  [plain(): pl.pallas_call(kernel, out_shape=shapes, in_specs=[vmem] * len(operands),...]
where the time goes in v4:
time: 123 us; the launch traced here: 122 us
  Pallas kernels  67.1 us (55%)
  waiting for transfers between devices  22.8 us (19%)
  starting transfers between devices  18.6 us (15%)
  local copies, waits for them, and re-layouts  9.59 us (8%)
  other arithmetic  3.32 us (3%)
    pallas_call x1, Pallas kernels, combine(): pl.pallas_call(functools.partial(combine_kernel, chunks, len(first), coun...  38.2 us
    pallas_call x2, Pallas kernels, plain(): pl.pallas_call(kernel, out_shape=shapes, in_specs=[vmem] * len(operands),...  28.9 us
    ppermute x6, waiting for transfers between devices, padded(): after = lax.ppermute(initial, axis, down)  20 us
    ppermute x6, starting transfers between devices, padded(): before = lax.ppermute(last, axis, up)  11.8 us
    ppermute x6, starting transfers between devices, padded(): after = lax.ppermute(initial, axis, down)  6.81 us
    slice x6, local copies, waits for them, and re-layouts, padded(): last = lax.slice_in_dim(array, length - width, length, axis=dim)  5.1 us
    ppermute x6, waiting for transfers between devices, padded(): before = lax.ppermute(last, axis, up)  2.77 us
    unnamed x15, local copies, waits for them, and re-layouts  2.58 us
  transfers between devices with their start and end apart: 12, of which 3 were waited for; matrix products, arithmetic and copies ran while one was open for 4% of the time, Pallas kernels for 2%

profile of v4, /device:TPU:0, one launch (start us, length us, event | category | flops | bytes accessed | tf_op | source)
XLA Modules:
  0.0 122.3 jit_solution(1743409821353677127)
XLA Ops:
  0.7 0.9 fusion.22
  2.0 2.0 %collective-permute-start.5 = (f32[3,2,8,128]{3,2,1,0:T(8,128)S(1)}, f32[3,2,8,128]{3,2,1,0:T(8,128)S(1)}, u32[]{:S(2)}, u32[]{:S(2)}) collective-permute-start(f32[3,2,8,128]{3,2,1,0:T(8,128)S(1)} %get-tuple-element.39), channel_id=1, source_target_pairs={{4,0},{8,4},{12,8},{0,12},{5,1},{9,5},{13,9},{1,13},{6,2},{10,6},{... | collective-permute-start | bytes 73736 | tf_op jit(solution)/shard_map/ppermute | solution.py:27
  4.0 1.9 %fusion.20 = (f32[3,32,2,128]{3,2,1,0:T(2,128)}, f32[3,32,2,128]{3,2,1,0:T(2,128)}) fusion(f32[3,32,8,128]{3,2,1,0:T(8,128)} %param.4), kind=kLoop, calls=%fused_computation.65 | loop fusion | bytes 393216 | tf_op jit(solution)/shard_map/slice | solution.py:24
  5.8 2.3 %collective-permute-start = (f32[3,32,2,128]{3,2,1,0:T(2,128)}, f32[3,32,2,128]{3,2,1,0:T(2,128)}, u32[]{:S(2)}, u32[]{:S(2)}) collective-permute-start(f32[3,32,2,128]{3,2,1,0:T(2,128)} %get-tuple-element.30), channel_id=1, source_target_pairs={{0,16},{16,0},{1,17},{17,1},{2,18},{18,2},{3,19},{19,3},{4,20},{20... | collective-permute-start | bytes 294920 | tf_op jit(solution)/shard_map/ppermute | solution.py:26
  8.2 2.1 %fusion.21 = (f32[3,32,8,2]{3,2,1,0:T(8,128)}, f32[3,32,8,2]{3,2,1,0:T(8,128)}) fusion(f32[3,32,8,128]{3,2,1,0:T(8,128)} %param.4), kind=kLoop, calls=%fused_computation.66 | loop fusion | bytes 24576 | tf_op jit(solution)/shard_map/slice | solution.py:24
  10.3 4.7 %collective-permute-start.2 = (f32[3,32,8,2]{3,2,1,0:T(8,128)}, f32[3,32,8,2]{3,2,1,0:T(8,128)}, u32[]{:S(2)}, u32[]{:S(2)}) collective-permute-start(f32[3,32,8,2]{3,2,1,0:T(8,128)} %get-tuple-element.36), channel_id=1, source_target_pairs={{0,1},{1,2},{2,3},{4,5},{5,6},{6,7},{8,9},{9,10},{10,11},{12,13},{... | collective-permute-start | bytes 18440 | tf_op jit(solution)/shard_map/ppermute | solution.py:26
  15.2 2.3 %modes_gram.1.refs_0_ = f32[1280,128]{1,0:T(8,128)S(1)} custom-call(f32[768,512]{1,0:T(8,128)S(1)} %copy-done), custom_call_target="tpu_custom_call" | custom-call | tf_op jit(solution)/shard_map/modes_gram/pallas_call | solution.py:373
  17.5 1.3 %collective-permute-start.3 = (f32[3,32,8,2]{3,2,1,0:T(8,128)S(1)}, f32[3,32,8,2]{3,2,1,0:T(8,128)S(1)}, u32[]{:S(2)}, u32[]{:S(2)}) collective-permute-start(f32[3,32,8,2]{3,2,1,0:T(8,128)S(1)} %copy-done.3), channel_id=1, source_target_pairs={{1,0},{2,1},{3,2},{5,4},{6,5},{7,6},{9,8},{10,9},{11,10},{13,12},{... | collective-permute-start | bytes 18440 | tf_op jit(solution)/shard_map/ppermute | solution.py:27
  19.0 10.5 %collective-permute-done.3 = f32[3,32,8,2]{3,2,1,0:T(8,128)S(1)} collective-permute-done((f32[3,32,8,2]{3,2,1,0:T(8,128)S(1)}, f32[3,32,8,2]{3,2,1,0:T(8,128)S(1)}, u32[]{:S(2)}, u32[]{:S(2)}) %collective-permute-start.3) | collective-permute-done | bytes 6176 | tf_op jit(solution)/shard_map/ppermute | solution.py:27
  29.5 0.9 constant_dynamic-update-slice_fusion
  30.5 2.1 %multiply_add_fusion = (f32[3,32,8,128]{3,2,1,0:T(8,128)S(1)}, f32[3,32,8,128]{3,2,1,0:T(8,128)S(1)}) fusion(f32[3,32,8,128]{3,2,1,0:T(8,128)S(1)} %copy-done.1, f32[32,8,128]{2,1,0:T(8,128)S(1)} %get-tuple-element.42, f32[32,8,128]{2,1,0:T(8,128)S(1)} %get-tuple-element.41, f32[32,8,128]{2,1,0:T(8,128)S(1)} %get-tuple-element.40, ...), kind=kLoop, calls=%fused_computation.42 | loop fusion | flops 5111808 | bytes 4823040 | tf_op jit(solution)/shard_map/add | solution.py:410
  32.9 2.8 %collective-permute-start.8 = (f32[3,32,8,2]{3,2,1,0:T(8,128)S(1)}, f32[3,32,8,2]{3,2,1,0:T(8,128)S(1)}, u32[]{:S(2)}, u32[]{:S(2)}) collective-permute-start(f32[3,32,8,2]{3,2,1,0:T(8,128)S(1)} %get-tuple-element.26), channel_id=1, source_target_pairs={{0,1},{1,2},{2,3},{4,5},{5,6},{6,7},{8,9},{9,10},{10,11},{12,13},{... | collective-permute-start | bytes 18440 | tf_op jit(solution)/shard_map/ppermute | solution.py:26
  35.7 1.7 %collective-permute-start.11 = (f32[3,2,8,128]{3,2,1,0:T(8,128)S(1)}, f32[3,2,8,128]{3,2,1,0:T(8,128)S(1)}, u32[]{:S(2)}, u32[]{:S(2)}) collective-permute-start(f32[3,2,8,128]{3,2,1,0:T(8,128)S(1)} %get-tuple-element.29), channel_id=1, source_target_pairs={{4,0},{8,4},{12,8},{0,12},{5,1},{9,5},{13,9},{1,13},{6,2},{10,6},{... | collective-permute-start | bytes 73736 | tf_op jit(solution)/shard_map/ppermute | solution.py:27
  37.5 1.5 %collective-permute-start.6 = (f32[3,32,2,128]{3,2,1,0:T(2,128)S(1)}, f32[3,32,2,128]{3,2,1,0:T(2,128)S(1)}, u32[]{:S(2)}, u32[]{:S(2)}) collective-permute-start(f32[3,32,2,128]{3,2,1,0:T(2,128)S(1)} %get-tuple-element.24), channel_id=1, source_target_pairs={{0,16},{16,0},{1,17},{17,1},{2,18},{18,2},{3,19},{19,3},{4,20},{20... | collective-permute-start | bytes 294920 | tf_op jit(solution)/shard_map/ppermute | solution.py:26
  39.0 0.5 collective-permute-start.7
  39.5 2.8 %collective-permute-done.8 = f32[3,32,8,2]{3,2,1,0:T(8,128)S(1)} collective-permute-done((f32[3,32,8,2]{3,2,1,0:T(8,128)S(1)}, f32[3,32,8,2]{3,2,1,0:T(8,128)S(1)}, u32[]{:S(2)}, u32[]{:S(2)}) %collective-permute-start.8) | collective-permute-done | bytes 6176 | tf_op jit(solution)/shard_map/ppermute | solution.py:26
  42.2 1.3 %collective-permute-start.9 = (f32[3,32,8,2]{3,2,1,0:T(8,128)S(1)}, f32[3,32,8,2]{3,2,1,0:T(8,128)S(1)}, u32[]{:S(2)}, u32[]{:S(2)}) collective-permute-start(f32[3,32,8,2]{3,2,1,0:T(8,128)S(1)} %get-tuple-element.27), channel_id=1, source_target_pairs={{1,0},{2,1},{3,2},{5,4},{6,5},{7,6},{9,8},{10,9},{11,10},{13,12},{... | collective-permute-start | bytes 18440 | tf_op jit(solution)/shard_map/ppermute | solution.py:27
  43.6 9.5 %collective-permute-done.9 = f32[3,32,8,2]{3,2,1,0:T(8,128)S(1)} collective-permute-done((f32[3,32,8,2]{3,2,1,0:T(8,128)S(1)}, f32[3,32,8,2]{3,2,1,0:T(8,128)S(1)}, u32[]{:S(2)}, u32[]{:S(2)}) %collective-permute-start.9) | collective-permute-done | bytes 6176 | tf_op jit(solution)/shard_map/ppermute | solution.py:27
  53.1 1.1 fusion.11
  54.2 0.7 copy-done.2
  55.2 0.6 gather_fusion
  55.8 38.2 %combine.1 = (f32[1280,128]{1,0:T(8,128)S(1)}, f32[512,128]{1,0:T(8,128)S(1)}, f32[128,768]{1,0:T(8,128)S(1)}) custom-call(f32[1280,128]{1,0:T(8,128)S(1)} %modes_gram.1.refs_0_, f32[4,32,768]{2,1,0:T(8,128)S(1)} %gather_fusion, f32[768,512]{1,0:T(8,128)S(1)} %copy-done, s32[128,1]{1,0:T(8,128)S(1)} %copy.11.refs_3_), custom_call_target="tpu_custom_call" | custom-call | tf_op jit(solution)/shard_map/combine/pallas_call | solution.py:261
  94.0 26.6 %factorize.1 = (f32[768,576]{1,0:T(8,128)S(1)}, f32[576,576]{1,0:T(8,128)}) custom-call(f32[1280,128]{1,0:T(8,128)S(1)} %get-tuple-element.8.first_ref, f32[512,128]{1,0:T(8,128)S(1)} %get-tuple-element.9.second_ref, f32[768,512]{1,0:T(8,128)S(1)} %copy-done, f32[128,768]{1,0:T(8,128)S(1)} %get-tuple-element.10.rows_ref), custom_call_target="tpu_custom_call" | custom-call | tf_op jit(solution)/shard_map/factorize/pallas_call | solution.py:373
  120.6 1.7 %copy.12 = f32[768,576]{0,1:T(8,128)} copy(f32[768,576]{1,0:T(8,128)S(1)} %get-tuple-element.17) | data formatting | bytes 3538944
  (38 shorter events, 1.4 us)
Async XLA Ops:
  0.6 14.4 %copy-start.1 = (f32[3,32,8,128]{3,2,1,0:T(8,128)S(1)}, f32[3,32,8,128]{3,2,1,0:T(8,128)}, u32[]{:S(2)}) copy-start(f32[3,32,8,128]{3,2,1,0:T(8,128)} %param.4) | copy-start | bytes 1179652
  0.6 14.4 %copy-start.4 = (s32[4]{0:T(128)S(1)}, s32[4]{0:T(128)}, u32[]{:S(2)}) copy-start(s32[4]{0:T(128)} %param.7) | copy-start | bytes 52
  0.7 14.4 %copy-start.5 = (s32[64]{0:T(128)S(1)}, s32[64]{0:T(128)}, u32[]{:S(2)}) copy-start(s32[64]{0:T(128)} %param.6) | copy-start | bytes 772
  0.7 14.5 %copy-start = (f32[768,512]{1,0:T(8,128)S(1)}, f32[768,512]{1,0:T(8,128)}, u32[]{:S(2)}) copy-start(f32[768,512]{1,0:T(8,128)} %modes_ref.3) | copy-start | bytes 4718596
  1.6 15.9 %collective-permute-start.4 = (f32[3,2,8,128]{3,2,1,0:T(8,128)S(1)}, f32[3,2,8,128]{3,2,1,0:T(8,128)S(1)}, u32[]{:S(2)}, u32[]{:S(2)}) collective-permute-start(f32[3,2,8,128]{3,2,1,0:T(8,128)S(1)} %get-tuple-element.38), channel_id=1, source_target_pairs={{0,4},{4,8},{8,12},{12,0},{1,5},{5,9},{9,13},{13,1},{2,6},{6,10},{... | collective-permute-start | bytes 73736 | tf_op jit(solution)/shard_map/ppermute | solution.py:26
  2.0 27.5 %collective-permute-start.5 = (f32[3,2,8,128]{3,2,1,0:T(8,128)S(1)}, f32[3,2,8,128]{3,2,1,0:T(8,128)S(1)}, u32[]{:S(2)}, u32[]{:S(2)}) collective-permute-start(f32[3,2,8,128]{3,2,1,0:T(8,128)S(1)} %get-tuple-element.39), channel_id=1, source_target_pairs={{4,0},{8,4},{12,8},{0,12},{5,1},{9,5},{13,9},{1,13},{6,2},{10,6},{... | collective-permute-start | bytes 73736 | tf_op jit(solution)/shard_map/ppermute | solution.py:27
  5.8 24.6 %collective-permute-start = (f32[3,32,2,128]{3,2,1,0:T(2,128)}, f32[3,32,2,128]{3,2,1,0:T(2,128)}, u32[]{:S(2)}, u32[]{:S(2)}) collective-permute-start(f32[3,32,2,128]{3,2,1,0:T(2,128)} %get-tuple-element.30), channel_id=1, source_target_pairs={{0,16},{16,0},{1,17},{17,1},{2,18},{18,2},{3,19},{19,3},{4,20},{20... | collective-permute-start | bytes 294920 | tf_op jit(solution)/shard_map/ppermute | solution.py:26
  8.1 21.4 %collective-permute-start.1 = (f32[3,32,2,128]{3,2,1,0:T(2,128)}, f32[3,32,2,128]{3,2,1,0:T(2,128)}, u32[]{:S(2)}, u32[]{:S(2)}) collective-permute-start(f32[3,32,2,128]{3,2,1,0:T(2,128)} %get-tuple-element.31), channel_id=1, source_target_pairs={{16,0},{0,16},{17,1},{1,17},{18,2},{2,18},{19,3},{3,19},{20,4},{4,... | collective-permute-start | bytes 294920 | tf_op jit(solution)/shard_map/ppermute | solution.py:27
  10.3 20.2 %collective-permute-start.2 = (f32[3,32,8,2]{3,2,1,0:T(8,128)}, f32[3,32,8,2]{3,2,1,0:T(8,128)}, u32[]{:S(2)}, u32[]{:S(2)}) collective-permute-start(f32[3,32,8,2]{3,2,1,0:T(8,128)} %get-tuple-element.36), channel_id=1, source_target_pairs={{0,1},{1,2},{2,3},{4,5},{5,6},{6,7},{8,9},{9,10},{10,11},{12,13},{... | collective-permute-start | bytes 18440 | tf_op jit(solution)/shard_map/ppermute | solution.py:26
  15.2 2.3 %copy-start.3 = (f32[3,32,8,2]{3,2,1,0:T(8,128)S(1)}, f32[3,32,8,2]{3,2,1,0:T(8,128)}, u32[]{:S(2)}) copy-start(f32[3,32,8,2]{3,2,1,0:T(8,128)} %get-tuple-element.37) | copy-start | bytes 18436
  17.5 11.9 %collective-permute-start.3 = (f32[3,32,8,2]{3,2,1,0:T(8,128)S(1)}, f32[3,32,8,2]{3,2,1,0:T(8,128)S(1)}, u32[]{:S(2)}, u32[]{:S(2)}) collective-permute-start(f32[3,32,8,2]{3,2,1,0:T(8,128)S(1)} %copy-done.3), channel_id=1, source_target_pairs={{1,0},{2,1},{3,2},{5,4},{6,5},{7,6},{9,8},{10,9},{11,10},{13,12},{... | collective-permute-start | bytes 18440 | tf_op jit(solution)/shard_map/ppermute | solution.py:27
  32.9 9.4 %collective-permute-start.8 = (f32[3,32,8,2]{3,2,1,0:T(8,128)S(1)}, f32[3,32,8,2]{3,2,1,0:T(8,128)S(1)}, u32[]{:S(2)}, u32[]{:S(2)}) collective-permute-start(f32[3,32,8,2]{3,2,1,0:T(8,128)S(1)} %get-tuple-element.26), channel_id=1, source_target_pairs={{0,1},{1,2},{2,3},{4,5},{5,6},{6,7},{8,9},{9,10},{10,11},{12,13},{... | collective-permute-start | bytes 18440 | tf_op jit(solution)/shard_map/ppermute | solution.py:26
  35.7 17.4 %collective-permute-start.10 = (f32[3,2,8,128]{3,2,1,0:T(8,128)S(1)}, f32[3,2,8,128]{3,2,1,0:T(8,128)S(1)}, u32[]{:S(2)}, u32[]{:S(2)}) collective-permute-start(f32[3,2,8,128]{3,2,1,0:T(8,128)S(1)} %get-tuple-element.28), channel_id=1, source_target_pairs={{0,4},{4,8},{8,12},{12,0},{1,5},{5,9},{9,13},{13,1},{2,6},{6,10},{... | collective-permute-start | bytes 73736 | tf_op jit(solution)/shard_map/ppermute | solution.py:26
  35.7 17.4 %collective-permute-start.11 = (f32[3,2,8,128]{3,2,1,0:T(8,128)S(1)}, f32[3,2,8,128]{3,2,1,0:T(8,128)S(1)}, u32[]{:S(2)}, u32[]{:S(2)}) collective-permute-start(f32[3,2,8,128]{3,2,1,0:T(8,128)S(1)} %get-tuple-element.29), channel_id=1, source_target_pairs={{4,0},{8,4},{12,8},{0,12},{5,1},{9,5},{13,9},{1,13},{6,2},{10,6},{... | collective-permute-start | bytes 73736 | tf_op jit(solution)/shard_map/ppermute | solution.py:27
  37.5 15.6 %collective-permute-start.6 = (f32[3,32,2,128]{3,2,1,0:T(2,128)S(1)}, f32[3,32,2,128]{3,2,1,0:T(2,128)S(1)}, u32[]{:S(2)}, u32[]{:S(2)}) collective-permute-start(f32[3,32,2,128]{3,2,1,0:T(2,128)S(1)} %get-tuple-element.24), channel_id=1, source_target_pairs={{0,16},{16,0},{1,17},{17,1},{2,18},{18,2},{3,19},{19,3},{4,20},{20... | collective-permute-start | bytes 294920 | tf_op jit(solution)/shard_map/ppermute | solution.py:26
  39.0 14.1 %collective-permute-start.7 = (f32[3,32,2,128]{3,2,1,0:T(2,128)S(1)}, f32[3,32,2,128]{3,2,1,0:T(2,128)S(1)}, u32[]{:S(2)}, u32[]{:S(2)}) collective-permute-start(f32[3,32,2,128]{3,2,1,0:T(2,128)S(1)} %get-tuple-element.25), channel_id=1, source_target_pairs={{16,0},{0,16},{17,1},{1,17},{18,2},{2,18},{19,3},{3,19},{20,4},{4,... | collective-permute-start | bytes 294920 | tf_op jit(solution)/shard_map/ppermute | solution.py:27
  42.2 10.8 %collective-permute-start.9 = (f32[3,32,8,2]{3,2,1,0:T(8,128)S(1)}, f32[3,32,8,2]{3,2,1,0:T(8,128)S(1)}, u32[]{:S(2)}, u32[]{:S(2)}) collective-permute-start(f32[3,32,8,2]{3,2,1,0:T(8,128)S(1)} %get-tuple-element.27), channel_id=1, source_target_pairs={{1,0},{2,1},{3,2},{5,4},{6,5},{7,6},{9,8},{10,9},{11,10},{13,12},{... | collective-permute-start | bytes 18440 | tf_op jit(solution)/shard_map/ppermute | solution.py:27
  54.2 0.7 copy-start.2

commit v5 on v4

--- a/solution.py
+++ b/solution.py
@@ -23,8 +23,15 @@
         down = [(j, i) for i, j in up]
         last = lax.slice_in_dim(array, length - width, length, axis=dim)
         initial = lax.slice_in_dim(array, 0, width, axis=dim)
+        if dim == array.ndim - 1:
+            shape = (width,) + array.shape[:-1]
+            last = jnp.moveaxis(last, -1, 0).reshape(width, -1)
+            initial = jnp.moveaxis(initial, -1, 0).reshape(width, -1)
         before = lax.ppermute(last, axis, up)
         after = lax.ppermute(initial, axis, down)
+        if dim == array.ndim - 1:
+            before = jnp.moveaxis(before.reshape(shape), 0, -1)
+            after = jnp.moveaxis(after.reshape(shape), 0, -1)
         array = jnp.concatenate([before, array, after], axis=dim)
     return array
 

time: 123 us -> 121 us (0.984)
  waiting for transfers between devices: 22.8 us -> 20 us
    ppermute x6, waiting for transfers between devices: 20 us -> 10.4 us  [padded(): after = lax.ppermute(initial, axis, down)]
    ppermute x6, waiting for transfers between devices: 2.77 us -> 9.61 us  [padded(): before = lax.ppermute(last, axis, up)]
  transfers between devices with their start and end apart: 12 -> 12, of which waited for: 3 -> 4; matrix products, arithmetic and copies ran while one was open for 4% -> 4% of each run, Pallas kernels for 2% -> 2%
where the time goes in v5:
time: 121 us
  Pallas kernels  67.2 us (56%)
  waiting for transfers between devices  20 us (17%)
  starting transfers between devices  19.4 us (16%)
  local copies, waits for them, and re-layouts  10.1 us (8%)
  other arithmetic  3.19 us (3%)
    pallas_call x1, Pallas kernels, combine(): pl.pallas_call(functools.partial(combine_kernel, chunks, len(first), coun...  38.3 us
    pallas_call x2, Pallas kernels, plain(): pl.pallas_call(kernel, out_shape=shapes, in_specs=[vmem] * len(operands),...  28.9 us
    ppermute x6, starting transfers between devices, padded(): before = lax.ppermute(last, axis, up)  12.6 us
    ppermute x6, waiting for transfers between devices, padded(): after = lax.ppermute(initial, axis, down)  10.4 us
    ppermute x6, waiting for transfers between devices, padded(): before = lax.ppermute(last, axis, up)  9.61 us
    ppermute x6, starting transfers between devices, padded(): after = lax.ppermute(initial, axis, down)  6.77 us
    slice x6, local copies, waits for them, and re-layouts, padded(): last = lax.slice_in_dim(array, length - width, length, axis=dim)  5.7 us
    unnamed x15, local copies, waits for them, and re-layouts  2.54 us
  transfers between devices with their start and end apart: 12, of which 4 were waited for; matrix products, arithmetic and copies ran while one was open for 4% of the time, Pallas kernels for 2%

profile of v5, /device:TPU:0, one launch (start us, length us, event | category | flops | bytes accessed | tf_op | source)
XLA Modules:
  0.0 120.8 jit_solution(12161034410922145381)
XLA Ops:
  0.7 1.5 %fusion.25 = (f32[3,2,8,128]{3,2,1,0:T(8,128)}, f32[3,2,8,128]{3,2,1,0:T(8,128)S(1)}) fusion(f32[3,32,8,128]{3,2,1,0:T(8,128)} %param.4), kind=kLoop, calls=%fused_computation.72 | loop fusion | bytes 98304 | tf_op jit(solution)/shard_map/slice | solution.py:24
  2.6 1.9 %collective-permute-start.5 = (f32[3,2,8,128]{3,2,1,0:T(8,128)S(1)}, f32[3,2,8,128]{3,2,1,0:T(8,128)S(1)}, u32[]{:S(2)}, u32[]{:S(2)}) collective-permute-start(f32[3,2,8,128]{3,2,1,0:T(8,128)S(1)} %get-tuple-element.38), channel_id=1, source_target_pairs={{4,0},{8,4},{12,8},{0,12},{5,1},{9,5},{13,9},{1,13},{6,2},{10,6},{... | collective-permute-start | bytes 73736 | tf_op jit(solution)/shard_map/ppermute | solution.py:31
  4.6 1.9 %fusion.23 = (f32[3,32,2,128]{3,2,1,0:T(2,128)}, f32[3,32,2,128]{3,2,1,0:T(2,128)}) fusion(f32[3,32,8,128]{3,2,1,0:T(8,128)} %param.4), kind=kLoop, calls=%fused_computation.70 | loop fusion | bytes 393216 | tf_op jit(solution)/shard_map/slice | solution.py:24
  6.4 2.3 %collective-permute-start = (f32[3,32,2,128]{3,2,1,0:T(2,128)}, f32[3,32,2,128]{3,2,1,0:T(2,128)}, u32[]{:S(2)}, u32[]{:S(2)}) collective-permute-start(f32[3,32,2,128]{3,2,1,0:T(2,128)} %get-tuple-element.30), channel_id=1, source_target_pairs={{0,16},{16,0},{1,17},{17,1},{2,18},{18,2},{3,19},{19,3},{4,20},{20... | collective-permute-start | bytes 294920 | tf_op jit(solution)/shard_map/ppermute | solution.py:30
  8.8 2.1 %fusion.24 = (f32[3,32,8,2]{3,2,1,0:T(8,128)}, f32[3,32,8,2]{3,2,1,0:T(8,128)}) fusion(f32[3,32,8,128]{3,2,1,0:T(8,128)} %param.4), kind=kLoop, calls=%fused_computation.71 | loop fusion | bytes 24576 | tf_op jit(solution)/shard_map/slice | solution.py:24
  10.9 1.3 %collective-permute-start.3 = (f32[2,768]{0,1:T(8,128)}, f32[2,768]{0,1:T(8,128)S(1)}, u32[]{:S(2)}, u32[]{:S(2)}) collective-permute-start(f32[2,768]{0,1:T(8,128)} %bitcast.5), channel_id=1, source_target_pairs={{1,0},{2,1},{3,2},{5,4},{6,5},{7,6},{9,8},{10,9},{11,10},{13,12},{... | collective-permute-start | bytes 18440 | tf_op jit(solution)/shard_map/ppermute | solution.py:31
  12.4 2.3 %modes_gram.1.refs_0_ = f32[1280,128]{1,0:T(8,128)S(1)} custom-call(f32[768,512]{1,0:T(8,128)S(1)} %copy-done), custom_call_target="tpu_custom_call" | custom-call | tf_op jit(solution)/shard_map/modes_gram/pallas_call | solution.py:380
  14.7 4.6 %collective-permute-start.2 = (f32[2,768]{0,1:T(8,128)S(1)}, f32[2,768]{0,1:T(8,128)S(1)}, u32[]{:S(2)}, u32[]{:S(2)}) collective-permute-start(f32[2,768]{0,1:T(8,128)S(1)} %bitcast.46), channel_id=1, source_target_pairs={{0,1},{1,2},{2,3},{4,5},{5,6},{6,7},{8,9},{9,10},{10,11},{12,13},{... | collective-permute-start | bytes 18440 | tf_op jit(solution)/shard_map/ppermute | solution.py:30
  19.5 0.9 constant_dynamic-update-slice_fusion
  20.4 3.4 %collective-permute-done.3 = f32[2,768]{0,1:T(8,128)S(1)} collective-permute-done((f32[2,768]{0,1:T(8,128)}, f32[2,768]{0,1:T(8,128)S(1)}, u32[]{:S(2)}, u32[]{:S(2)}) %collective-permute-start.3) | collective-permute-done | bytes 6176 | tf_op jit(solution)/shard_map/ppermute | solution.py:31
  23.8 3.5 %collective-permute-done.2 = f32[2,768]{0,1:T(8,128)S(1)} collective-permute-done((f32[2,768]{0,1:T(8,128)S(1)}, f32[2,768]{0,1:T(8,128)S(1)}, u32[]{:S(2)}, u32[]{:S(2)}) %collective-permute-start.2) | collective-permute-done | bytes 6176 | tf_op jit(solution)/shard_map/ppermute | solution.py:30
  27.3 2.0 %multiply_add_fusion = (f32[3,32,8,128]{3,2,1,0:T(8,128)S(1)}, f32[3,32,8,128]{3,2,1,0:T(8,128)S(1)}) fusion(f32[3,32,8,128]{3,2,1,0:T(8,128)S(1)} %copy-done.1, f32[32,8,128]{2,1,0:T(8,128)S(1)} %get-tuple-element.41, f32[32,8,128]{2,1,0:T(8,128)S(1)} %get-tuple-element.40, f32[32,8,128]{2,1,0:T(8,128)S(1)} %get-tuple-element.39, ...), kind=kLoop, calls=%fused_computation.46 | loop fusion | flops 5308416 | bytes 4042752 | tf_op jit(solution)/shard_map/add | solution.py:417
  29.5 1.3 %collective-permute-start.9 = (f32[2,768]{0,1:T(8,128)S(1)}, f32[2,768]{0,1:T(8,128)S(1)}, u32[]{:S(2)}, u32[]{:S(2)}) collective-permute-start(f32[2,768]{0,1:T(8,128)S(1)} %bitcast.48), channel_id=1, source_target_pairs={{1,0},{2,1},{3,2},{5,4},{6,5},{7,6},{9,8},{10,9},{11,10},{13,12},{... | collective-permute-start | bytes 18440 | tf_op jit(solution)/shard_map/ppermute | solution.py:31
  30.9 1.7 %collective-permute-start.11 = (f32[3,2,8,128]{3,2,1,0:T(8,128)S(1)}, f32[3,2,8,128]{3,2,1,0:T(8,128)S(1)}, u32[]{:S(2)}, u32[]{:S(2)}) collective-permute-start(f32[3,2,8,128]{3,2,1,0:T(8,128)S(1)} %get-tuple-element.29), channel_id=1, source_target_pairs={{4,0},{8,4},{12,8},{0,12},{5,1},{9,5},{13,9},{1,13},{6,2},{10,6},{... | collective-permute-start | bytes 73736 | tf_op jit(solution)/shard_map/ppermute | solution.py:31
  32.7 1.5 %collective-permute-start.6 = (f32[3,32,2,128]{3,2,1,0:T(2,128)S(1)}, f32[3,32,2,128]{3,2,1,0:T(2,128)S(1)}, u32[]{:S(2)}, u32[]{:S(2)}) collective-permute-start(f32[3,32,2,128]{3,2,1,0:T(2,128)S(1)} %get-tuple-element.24), channel_id=1, source_target_pairs={{0,16},{16,0},{1,17},{17,1},{2,18},{18,2},{3,19},{19,3},{4,20},{20... | collective-permute-start | bytes 294920 | tf_op jit(solution)/shard_map/ppermute | solution.py:30
  34.7 7.1 %collective-permute-done.9 = f32[2,768]{0,1:T(8,128)S(1)} collective-permute-done((f32[2,768]{0,1:T(8,128)S(1)}, f32[2,768]{0,1:T(8,128)S(1)}, u32[]{:S(2)}, u32[]{:S(2)}) %collective-permute-start.9) | collective-permute-done | bytes 6176 | tf_op jit(solution)/shard_map/ppermute | solution.py:31
  41.7 3.7 %collective-permute-start.8 = (f32[2,768]{0,1:T(8,128)S(1)}, f32[2,768]{0,1:T(8,128)S(1)}, u32[]{:S(2)}, u32[]{:S(2)}) collective-permute-start(f32[2,768]{0,1:T(8,128)S(1)} %bitcast.47), channel_id=1, source_target_pairs={{0,1},{1,2},{2,3},{4,5},{5,6},{6,7},{8,9},{9,10},{10,11},{12,13},{... | collective-permute-start | bytes 18440 | tf_op jit(solution)/shard_map/ppermute | solution.py:30
  45.4 6.1 %collective-permute-done.8 = f32[2,768]{0,1:T(8,128)S(1)} collective-permute-done((f32[2,768]{0,1:T(8,128)S(1)}, f32[2,768]{0,1:T(8,128)S(1)}, u32[]{:S(2)}, u32[]{:S(2)}) %collective-permute-start.8) | collective-permute-done | bytes 6176 | tf_op jit(solution)/shard_map/ppermute | solution.py:30
  51.5 1.1 fusion.12
  52.7 0.7 copy-done.2
  53.7 0.6 gather_fusion
  54.3 38.3 %combine.1 = (f32[1280,128]{1,0:T(8,128)S(1)}, f32[512,128]{1,0:T(8,128)S(1)}, f32[128,768]{1,0:T(8,128)S(1)}) custom-call(f32[1280,128]{1,0:T(8,128)S(1)} %modes_gram.1.refs_0_, f32[4,32,768]{2,1,0:T(8,128)S(1)} %gather_fusion, f32[768,512]{1,0:T(8,128)S(1)} %copy-done, s32[128,1]{1,0:T(8,128)S(1)} %copy.11.refs_3_), custom_call_target="tpu_custom_call" | custom-call | tf_op jit(solution)/shard_map/combine/pallas_call | solution.py:268
  92.6 26.6 %factorize.1 = (f32[768,576]{1,0:T(8,128)S(1)}, f32[576,576]{1,0:T(8,128)}) custom-call(f32[1280,128]{1,0:T(8,128)S(1)} %get-tuple-element.8.first_ref, f32[512,128]{1,0:T(8,128)S(1)} %get-tuple-element.9.second_ref, f32[768,512]{1,0:T(8,128)S(1)} %copy-done, f32[128,768]{1,0:T(8,128)S(1)} %get-tuple-element.10.rows_ref), custom_call_target="tpu_custom_call" | custom-call | tf_op jit(solution)/shard_map/factorize/pallas_call | solution.py:380
  119.2 1.7 %copy.12 = f32[768,576]{0,1:T(8,128)} copy(f32[768,576]{1,0:T(8,128)S(1)} %get-tuple-element.17) | data formatting | bytes 3538944
  (37 shorter events, 1.9 us)
Async XLA Ops:
  0.6 11.5 %copy-start.1 = (f32[3,32,8,128]{3,2,1,0:T(8,128)S(1)}, f32[3,32,8,128]{3,2,1,0:T(8,128)}, u32[]{:S(2)}) copy-start(f32[3,32,8,128]{3,2,1,0:T(8,128)} %param.4) | copy-start | bytes 1179652
  0.6 11.6 %copy-start.4 = (s32[4]{0:T(128)S(1)}, s32[4]{0:T(128)}, u32[]{:S(2)}) copy-start(s32[4]{0:T(128)} %param.7) | copy-start | bytes 52
  0.7 11.6 %copy-start.5 = (s32[64]{0:T(128)S(1)}, s32[64]{0:T(128)}, u32[]{:S(2)}) copy-start(s32[64]{0:T(128)} %param.6) | copy-start | bytes 772
  0.7 11.7 %copy-start = (f32[768,512]{1,0:T(8,128)S(1)}, f32[768,512]{1,0:T(8,128)}, u32[]{:S(2)}) copy-start(f32[768,512]{1,0:T(8,128)} %modes_ref.3) | copy-start | bytes 4718596
  2.2 12.5 %collective-permute-start.4 = (f32[3,2,8,128]{3,2,1,0:T(8,128)}, f32[3,2,8,128]{3,2,1,0:T(8,128)S(1)}, u32[]{:S(2)}, u32[]{:S(2)}) collective-permute-start(f32[3,2,8,128]{3,2,1,0:T(8,128)} %get-tuple-element.37), channel_id=1, source_target_pairs={{0,4},{4,8},{8,12},{12,0},{1,5},{5,9},{9,13},{13,1},{2,6},{6,10},{... | collective-permute-start | bytes 73736 | tf_op jit(solution)/shard_map/ppermute | solution.py:30
  2.6 16.8 %collective-permute-start.5 = (f32[3,2,8,128]{3,2,1,0:T(8,128)S(1)}, f32[3,2,8,128]{3,2,1,0:T(8,128)S(1)}, u32[]{:S(2)}, u32[]{:S(2)}) collective-permute-start(f32[3,2,8,128]{3,2,1,0:T(8,128)S(1)} %get-tuple-element.38), channel_id=1, source_target_pairs={{4,0},{8,4},{12,8},{0,12},{5,1},{9,5},{13,9},{1,13},{6,2},{10,6},{... | collective-permute-start | bytes 73736 | tf_op jit(solution)/shard_map/ppermute | solution.py:31
  6.4 20.9 %collective-permute-start = (f32[3,32,2,128]{3,2,1,0:T(2,128)}, f32[3,32,2,128]{3,2,1,0:T(2,128)}, u32[]{:S(2)}, u32[]{:S(2)}) collective-permute-start(f32[3,32,2,128]{3,2,1,0:T(2,128)} %get-tuple-element.30), channel_id=1, source_target_pairs={{0,16},{16,0},{1,17},{17,1},{2,18},{18,2},{3,19},{19,3},{4,20},{20... | collective-permute-start | bytes 294920 | tf_op jit(solution)/shard_map/ppermute | solution.py:30
  8.7 10.7 %collective-permute-start.1 = (f32[3,32,2,128]{3,2,1,0:T(2,128)}, f32[3,32,2,128]{3,2,1,0:T(2,128)}, u32[]{:S(2)}, u32[]{:S(2)}) collective-permute-start(f32[3,32,2,128]{3,2,1,0:T(2,128)} %get-tuple-element.31), channel_id=1, source_target_pairs={{16,0},{0,16},{17,1},{1,17},{18,2},{2,18},{19,3},{3,19},{20,4},{4,... | collective-permute-start | bytes 294920 | tf_op jit(solution)/shard_map/ppermute | solution.py:31
  10.9 12.9 %collective-permute-start.3 = (f32[2,768]{0,1:T(8,128)}, f32[2,768]{0,1:T(8,128)S(1)}, u32[]{:S(2)}, u32[]{:S(2)}) collective-permute-start(f32[2,768]{0,1:T(8,128)} %bitcast.5), channel_id=1, source_target_pairs={{1,0},{2,1},{3,2},{5,4},{6,5},{7,6},{9,8},{10,9},{11,10},{13,12},{... | collective-permute-start | bytes 18440 | tf_op jit(solution)/shard_map/ppermute | solution.py:31
  12.4 2.3 %copy-start.3 = (f32[3,32,8,2]{3,2,1,0:T(8,128)S(1)}, f32[3,32,8,2]{3,2,1,0:T(8,128)}, u32[]{:S(2)}) copy-start(f32[3,32,8,2]{3,2,1,0:T(8,128)} %get-tuple-element.35) | copy-start | bytes 18436
  14.7 12.6 %collective-permute-start.2 = (f32[2,768]{0,1:T(8,128)S(1)}, f32[2,768]{0,1:T(8,128)S(1)}, u32[]{:S(2)}, u32[]{:S(2)}) collective-permute-start(f32[2,768]{0,1:T(8,128)S(1)} %bitcast.46), channel_id=1, source_target_pairs={{0,1},{1,2},{2,3},{4,5},{5,6},{6,7},{8,9},{9,10},{10,11},{12,13},{... | collective-permute-start | bytes 18440 | tf_op jit(solution)/shard_map/ppermute | solution.py:30
  29.5 12.2 %collective-permute-start.9 = (f32[2,768]{0,1:T(8,128)S(1)}, f32[2,768]{0,1:T(8,128)S(1)}, u32[]{:S(2)}, u32[]{:S(2)}) collective-permute-start(f32[2,768]{0,1:T(8,128)S(1)} %bitcast.48), channel_id=1, source_target_pairs={{1,0},{2,1},{3,2},{5,4},{6,5},{7,6},{9,8},{10,9},{11,10},{13,12},{... | collective-permute-start | bytes 18440 | tf_op jit(solution)/shard_map/ppermute | solution.py:31
  30.9 20.7 %collective-permute-start.10 = (f32[3,2,8,128]{3,2,1,0:T(8,128)S(1)}, f32[3,2,8,128]{3,2,1,0:T(8,128)S(1)}, u32[]{:S(2)}, u32[]{:S(2)}) collective-permute-start(f32[3,2,8,128]{3,2,1,0:T(8,128)S(1)} %get-tuple-element.28), channel_id=1, source_target_pairs={{0,4},{4,8},{8,12},{12,0},{1,5},{5,9},{9,13},{13,1},{2,6},{6,10},{... | collective-permute-start | bytes 73736 | tf_op jit(solution)/shard_map/ppermute | solution.py:30
  30.9 20.6 %collective-permute-start.11 = (f32[3,2,8,128]{3,2,1,0:T(8,128)S(1)}, f32[3,2,8,128]{3,2,1,0:T(8,128)S(1)}, u32[]{:S(2)}, u32[]{:S(2)}) collective-permute-start(f32[3,2,8,128]{3,2,1,0:T(8,128)S(1)} %get-tuple-element.29), channel_id=1, source_target_pairs={{4,0},{8,4},{12,8},{0,12},{5,1},{9,5},{13,9},{1,13},{6,2},{10,6},{... | collective-permute-start | bytes 73736 | tf_op jit(solution)/shard_map/ppermute | solution.py:31
  32.7 18.9 %collective-permute-start.6 = (f32[3,32,2,128]{3,2,1,0:T(2,128)S(1)}, f32[3,32,2,128]{3,2,1,0:T(2,128)S(1)}, u32[]{:S(2)}, u32[]{:S(2)}) collective-permute-start(f32[3,32,2,128]{3,2,1,0:T(2,128)S(1)} %get-tuple-element.24), channel_id=1, source_target_pairs={{0,16},{16,0},{1,17},{17,1},{2,18},{18,2},{3,19},{19,3},{4,20},{20... | collective-permute-start | bytes 294920 | tf_op jit(solution)/shard_map/ppermute | solution.py:30
  34.2 17.3 %collective-permute-start.7 = (f32[3,32,2,128]{3,2,1,0:T(2,128)S(1)}, f32[3,32,2,128]{3,2,1,0:T(2,128)S(1)}, u32[]{:S(2)}, u32[]{:S(2)}) collective-permute-start(f32[3,32,2,128]{3,2,1,0:T(2,128)S(1)} %get-tuple-element.25), channel_id=1, source_target_pairs={{16,0},{0,16},{17,1},{1,17},{18,2},{2,18},{19,3},{3,19},{20,4},{4,... | collective-permute-start | bytes 294920 | tf_op jit(solution)/shard_map/ppermute | solution.py:31
  41.7 9.8 %collective-permute-start.8 = (f32[2,768]{0,1:T(8,128)S(1)}, f32[2,768]{0,1:T(8,128)S(1)}, u32[]{:S(2)}, u32[]{:S(2)}) collective-permute-start(f32[2,768]{0,1:T(8,128)S(1)} %bitcast.47), channel_id=1, source_target_pairs={{0,1},{1,2},{2,3},{4,5},{5,6},{6,7},{8,9},{9,10},{10,11},{12,13},{... | collective-permute-start | bytes 18440 | tf_op jit(solution)/shard_map/ppermute | solution.py:30
  52.7 0.7 copy-start.2
